TPU v7x, 128 devices: a whole 4x4x4 slice. The times are simulated.
128 devices in a mesh: gx: 4 (over y), gy: 32 (over z, x, core).
Axes of the slice: x: 4, y: 4, z: 4, core: 2. Of those that a mesh axis runs over, the one named last changes fastest.
Arguments:
- features: float32 [7, 1048576], P(None, ('gx', 'gy')), may hold values from -4 to 4
- first_slot: int32 [4096], P(('gx', 'gy')), may hold values from 0 to 7
- second_owner: int32 [4096, 1], P(('gx', 'gy')), may hold values from 0 to 31; in each aligned block of 32 rows (0 to 31, 32 to 63, ...) at most 2 rows name the same one
- second_slot: int32 [4096], P(('gx', 'gy')), may hold values from 0 to 7
- pair_count: int32 [128], P(('gx', 'gy')), may hold values from 1 to 32, as said below
Outputs:
- gradient: float32 [6, 1048576], P(None, ('gx', 'gy'))
- energy: float32 [], replicated
Inputs may be any that keep to these rules, and one draw needn't show every extreme that they name: `pair_count`: some device holds exactly 32 live entries. `second_owner`: among the 32 entries of one device, live or not, at most 2 name the same owner; in some devices one owner is named exactly 2 times.
All inputs are finite; a program needn't handle non-finite values.
Results may differ from a plain program's by a relative error of at most 0.0003.
Values sent between devices are 32-bit elements; how exact they have to be, the bound alone decides.
A program may use at most 64 MiB of HBM per device.

v0:
```python
import jax
import jax.numpy as jnp
from jax import lax
from jax.sharding import PartitionSpec as P

BLOCK = 1024


def contract_cols(left, right):
    return lax.dot_general(
        left,
        right,
        (((1,), (1,)), ((), ())),
        precision=lax.Precision.HIGHEST,
        preferred_element_type=jnp.float32,
    )


def contract_rows(left, right):
    return jnp.dot(left, right, precision=lax.Precision.HIGHEST, preferred_element_type=jnp.float32)


def tile_terms(first_block, second_block, factor):
    dist_sq = jnp.zeros((first_block.shape[1], second_block.shape[1]), jnp.float32)
    alignment = jnp.zeros((first_block.shape[1], second_block.shape[1]), jnp.float32)
    for coord in range(3):
        diff = first_block[coord][:, None] - second_block[coord][None, :]
        dist_sq = dist_sq + diff * diff
        alignment = alignment + first_block[3 + coord][:, None] * second_block[3 + coord][None, :]
    weights = first_block[6][:, None] * second_block[6][None, :]
    gaussian = jnp.exp(-0.5 * dist_sq)
    kernel = weights * gaussian * alignment * alignment
    energy = factor * jnp.sum(kernel)
    pulling = -factor * kernel
    turning = 2.0 * factor * weights * gaussian * alignment
    first_pos = first_block[0:3]
    second_pos = second_block[0:3]
    grad_first = jnp.concatenate(
        [
            first_pos * jnp.sum(pulling, axis=1)[None, :] - contract_cols(second_pos, pulling),
            contract_cols(second_block[3:6], turning),
        ],
        axis=0,
    )
    grad_second = jnp.concatenate(
        [
            second_pos * jnp.sum(pulling, axis=0)[None, :] - contract_rows(first_pos, pulling),
            contract_rows(first_block[3:6], turning),
        ],
        axis=0,
    )
    return (grad_first, grad_second, energy)


def shards(features, first_slot, second_owner, second_slot, pair_count):
    block_width = BLOCK
    owned = features.shape[1] // block_width
    blocks = features.reshape(7, owned, block_width).transpose(1, 0, 2)
    entries = first_slot.shape[0]
    groups = lax.axis_size("gy")
    capacity = max(2, entries // groups)
    self_index = lax.axis_index("gy")
    live_count = pair_count[0]
    owners = second_owner[:, 0]
    live = jnp.arange(entries, dtype=jnp.int32) < live_count
    factors = jnp.where((owners == self_index) & (second_slot == first_slot), 1.0, 2.0).astype(
        jnp.float32
    )
    local_grads = jnp.zeros((owned, 6, block_width), jnp.float32)
    energy_init = jnp.zeros((), jnp.float32)
    owner_hits = (owners[:, None] == jnp.arange(groups, dtype=jnp.int32)[None, :]) & live[:, None]
    running = jnp.cumsum(owner_hits.astype(jnp.int32), axis=0) - 1
    order_rank = jnp.sum(jnp.where(owner_hits, running, 0), axis=1)
    slot_index = owners * capacity + order_rank
    slot_table = (
        slot_index[:, None] == jnp.arange(groups * capacity, dtype=jnp.int32)[None, :]
    ) & live[:, None]
    wanted = jnp.sum(jnp.where(slot_table, second_slot[:, None] + 1, 0), axis=0) - 1
    requested = lax.all_to_all(
        wanted.reshape(groups, capacity), "gy", split_axis=0, concat_axis=0, tiled=True
    ).reshape(groups * capacity)
    valid = (requested >= 0).astype(jnp.float32)
    outgoing = blocks[jnp.clip(requested, 0, owned - 1)] * valid[:, None, None]
    fetched = lax.all_to_all(
        outgoing.reshape(groups, capacity, 7, block_width),
        "gy",
        split_axis=0,
        concat_axis=0,
        tiled=True,
    ).reshape(groups * capacity, 7, block_width)

    def visit_entry(entry_index, carried):
        grads_now, returned, energy_now = carried
        grad_first, grad_second, energy = tile_terms(
            blocks[first_slot[entry_index]], fetched[slot_index[entry_index]], factors[entry_index]
        )
        grads_now = grads_now.at[first_slot[entry_index]].add(grad_first)
        returned = returned.at[slot_index[entry_index]].add(grad_second)
        return (grads_now, returned, energy_now + energy)

    returned_init = jnp.zeros((groups * capacity, 6, block_width), jnp.float32)
    local_grads, returned, energy_local = lax.fori_loop(
        0, live_count, visit_entry, (local_grads, returned_init, energy_init)
    )
    arrived = lax.all_to_all(
        returned.reshape(groups, capacity, 6, block_width),
        "gy",
        split_axis=0,
        concat_axis=0,
        tiled=True,
    ).reshape(groups * capacity, 6, block_width)
    selector = (requested[:, None] == jnp.arange(owned, dtype=jnp.int32)[None, :]).astype(
        jnp.float32
    )
    local_grads = local_grads + jnp.einsum(
        "sl,sfb->lfb", selector, arrived, precision=lax.Precision.HIGHEST
    )
    total = lax.psum(energy_local, ("gx", "gy"))
    gradient = local_grads.transpose(1, 0, 2).reshape(6, owned * block_width)
    return (gradient, total / block_width)


def solution(mesh):
    return jax.shard_map(
        shards,
        mesh=mesh,
        in_specs=(
            P(None, ("gx", "gy")),
            P(("gx", "gy")),
            P(("gx", "gy"), None),
            P(("gx", "gy")),
            P(("gx", "gy")),
        ),
        out_specs=(P(None, ("gx", "gy")), P()),
        check_vma=False,
    )
```

profile of v0, /device:TPU:1, one launch (start us, length us, event | category | flops | bytes accessed | tf_op | source)
XLA Modules:
  0.0 1532.0 jit_solution(8720694244024407151)
XLA Ops:
  4.5 16.2 %all_to_all.16 = s32[32,1,2]{2,1,0:T(1,128)S(1)} all-to-all(s32[32,1,2]{2,1,0:T(1,128)S(1)} %bitcast.207), channel_id=1, replica_groups=mesh['gx'=4,'gy'=32] {'gy'}, dimensions={0} | all-to-all | bytes 512 | tf_op jit(solution)/shard_map/all_to_all | solution.py:79
  30.5 24.9 %all-to-all-done.1 = f32[32,2,7,1024]{3,1,2,0:T(2,128)S(1)} async-done(((f32[32,2,7,1024]{3,1,2,0:T(2,128)}), f32[32,2,7,1024]{3,1,2,0:T(2,128)S(1)}, u32[]{:S(2)}, u32[]{:S(2)}) %all-to-all-start.1) | async-done | bytes 1835040 | tf_op jit(solution)/shard_map/all_to_all | solution.py:84
  58.3 865.9 %while.16 = (s32[]{:T(128)}, f32[8,6,1024]{2,0,1:T(8,128)S(1)}, f32[64,6,1024]{2,1,0:T(8,128)S(1)}, f32[]{:T(128)}, s32[]{:T(128)}, /*index=5*/s32[32]{0:T(128)S...) while((s32[]{:T(128)}, f32[8,6,1024]{2,0,1:T(8,128)S(1)}, ...), condition=%wide.region_9.10_spmd, body=%wide.region_3.9_spmd.sunk | while | flops 251705392 | bytes 888407 | solution.py:102
  74.5 7.1 fusion.53
  81.6 5.9 fusion.55
  93.3 6.9 fusion.51
  117.8 7.1 fusion.53
  124.9 5.9 fusion.55
  136.6 6.9 fusion.51
  161.0 7.1 fusion.53
  168.1 5.9 fusion.55
  179.8 6.9 fusion.51
  204.3 7.1 fusion.53
  211.3 5.9 fusion.55
  223.1 6.9 fusion.51
  247.5 7.1 fusion.53
  254.6 5.9 fusion.55
  266.3 6.9 fusion.51
  290.7 7.1 fusion.53
  297.8 5.9 fusion.55
  309.5 6.9 fusion.51
  333.9 7.1 fusion.53
  341.0 5.9 fusion.55
  352.8 6.9 fusion.51
  377.2 7.1 fusion.53
  384.2 5.9 fusion.55
  396.0 6.9 fusion.51
  420.4 7.1 fusion.53
  427.5 5.9 fusion.55
  439.2 6.9 fusion.51
  463.6 7.1 fusion.53
  470.7 5.9 fusion.55
  482.4 6.9 fusion.51
  506.9 7.1 fusion.53
  514.0 5.9 fusion.55
  525.7 6.9 fusion.51
  550.1 7.1 fusion.53
  557.2 5.9 fusion.55
  568.9 6.9 fusion.51
  593.3 7.1 fusion.53
  600.4 5.9 fusion.55
  612.2 6.9 fusion.51
  636.6 7.1 fusion.53
  643.6 5.9 fusion.55
  655.4 6.9 fusion.51
  680.0 7.1 fusion.53
  687.1 5.9 fusion.55
  698.8 6.9 fusion.51
  723.2 7.1 fusion.53
  730.3 5.9 fusion.55
  742.0 6.9 fusion.51
  766.4 7.1 fusion.53
  773.5 5.9 fusion.55
  785.3 6.9 fusion.51
  809.7 7.1 fusion.53
  828.5 6.9 fusion.51
  853.0 7.1 fusion.53
  860.0 5.9 fusion.55
  871.8 6.9 fusion.51
  896.2 7.1 fusion.53
  903.3 5.9 fusion.55
  915.0 6.9 fusion.51
  926.7 524.4 %all-to-all-start.2 = ((f32[32,2,6,1024]{3,1,2,0:T(2,128)}), f32[32,2,6,1024]{3,1,2,0:T(2,128)S(1)}, u32[]{:S(2)}, u32[]{:S(2)}) async-start(f32[32,2,6,1024]{3,1,2,0:T(2,128)} %copy.52), calls=%async_computation.2 | async-start | bytes 3145728 | tf_op jit(solution)/shard_map/all_to_all | solution.py:105
  1452.4 74.7 %psum.7 = f32[]{:T(128)} all-reduce(f32[]{:T(128)} %get-tuple-element.83), channel_id=1, replica_groups=mesh['gx'=4,'gy'=32] {'gx','gy'}, use_global_device_ids=true, to_apply=%region_10.11 | all-reduce | flops 1 | bytes 8 | tf_op jit(solution)/shard_map/psum | solution.py:118
  (286 shorter events, 361.3 us)
Async XLA Ops:
  26.0 4.4 copy-start.2
  26.1 4.5 copy-start.3
  26.1 4.5 copy-start.4
  26.1 29.4 %all-to-all-start.1 = ((f32[32,2,7,1024]{3,1,2,0:T(2,128)}), f32[32,2,7,1024]{3,1,2,0:T(2,128)S(1)}, u32[]{:S(2)}, u32[]{:S(2)}) async-start(f32[32,2,7,1024]{3,1,2,0:T(2,128)} %copy.48), calls=%async_computation.1 | async-start | bytes 3670016 | tf_op jit(solution)/shard_map/all_to_all | solution.py:84
  57.7 0.7 copy-start
  57.7 0.7 copy-start.1
  926.7 601.0 %all-to-all-start.2 = ((f32[32,2,6,1024]{3,1,2,0:T(2,128)}), f32[32,2,6,1024]{3,1,2,0:T(2,128)S(1)}, u32[]{:S(2)}, u32[]{:S(2)}) async-start(f32[32,2,6,1024]{3,1,2,0:T(2,128)} %copy.52), calls=%async_computation.2 | async-start | bytes 3145728 | tf_op jit(solution)/shard_map/all_to_all | solution.py:105
where the time goes:
time: 1550 us; the launch traced here: 1530 us
  starting transfers between devices  529 us (34%)
  matrix products  516 us (33%)
  other arithmetic  157 us (10%)
  loops' own time  134 us (9%)
  blocking collectives  90.8 us (6%)
  local copies, waits for them, and re-layouts  77.4 us (5%)
  waiting for transfers between devices  24.9 us (2%)
    all_to_all x1, starting transfers between devices, shards(): lax.all_to_all(returned.reshape(groups, capacity, 6, block_width), 'gy',...  524 us
    dot_general x40, matrix products, contract_cols(): lax.dot_general(left, right, (((1,), (1,)), ((), ())), precision=lax.Prec...  280 us
    dot_general x40, matrix products, contract_rows(): jnp.dot(left, right, precision=lax.Precision.HIGHEST, preferred_element_t...  235 us
    another operation x1, loops' own time, shards(): lax.fori_loop(0, live_count, visit_entry, (local_grads, returned_init, en...  134 us
    reduce_sum x20, other arithmetic, tile_terms(): energy = factor * jnp.sum(kernel)  112 us
    psum x1, blocking collectives, shards(): total = lax.psum(energy_local, ('gx', 'gy'))  74.7 us
  transfers between devices with their start and end apart: 2, of which 1 were waited for; matrix products, arithmetic and copies ran while one was open for 0% of the time, Pallas kernels for 0%

commit v1 on v0

v1 whole, which is shorter than its diff:
```python
import jax
import jax.numpy as jnp
from jax import lax
from jax.experimental import pallas as pl
from jax.experimental.pallas import tpu as pltpu
from jax.sharding import PartitionSpec as P

BLOCK = 1024
TILE = 256
LOG2E = 1.4426950408889634
F32 = jnp.float32
BF16 = jnp.bfloat16


def dot(left, right, left_dim, right_dim):
    return lax.dot_general(
        left, right, (((left_dim,), (right_dim,)), ((), ())), preferred_element_type=F32
    )


def split_three(value):
    high = value.astype(BF16).astype(F32)
    rest = value - high
    mid = rest.astype(BF16).astype(F32)
    return high, mid, rest - mid


def select_rows(rows):
    index = lax.broadcasted_iota(jnp.int32, (8, BLOCK), 0)
    tile = jnp.zeros((8, BLOCK), F32)
    for place, row in enumerate(rows):
        tile = jnp.where(index == place, row, tile)
    return tile


def read_rows(block):
    return [block[row : row + 1] for row in range(7)]


def exponent_rows(rows):
    x, y, z = rows[:3]
    norm = (-0.5 * LOG2E) * (x * x + y * y + z * z)
    one = jnp.ones_like(x)
    left = select_rows([LOG2E * x, LOG2E * y, LOG2E * z, one, norm])
    right = select_rows([x, y, z, norm, one])
    return left, right


def left_splits(left):
    high, mid, low = split_three(left)
    return jnp.concatenate([high, high, mid, mid, high, low], axis=0)


def right_splits(right):
    high, mid, low = split_three(right)
    return jnp.concatenate([high, mid, high, mid, low, high], axis=0).astype(BF16)


def normal_products(rows):
    nx, ny, nz = rows[3:6]
    return select_rows([nx, ny, nz, nx, nx, ny]) * select_rows([nx, ny, nz, ny, nz, nz])


def moment_rows(rows):
    x, y, z, w = rows[0], rows[1], rows[2], rows[6]
    base = normal_products(rows) * w
    full = jnp.concatenate([base, base * x, base * y, base * z], axis=0)
    high = full.astype(BF16)
    low = (full - high.astype(F32)).astype(BF16)
    return jnp.concatenate([high, low], axis=0)


def finish(rows, moments, factor):
    x, y, z, nx, ny, nz, w = rows
    index = lax.broadcasted_iota(jnp.int32, (8, BLOCK), 0)
    doubled = normal_products(rows) * jnp.where(index < 3, 1.0, 2.0)
    mass = w * factor
    m0 = moments[0:8]
    sums = [
        jnp.sum(doubled * moments[8 * part : 8 * part + 8], axis=0, keepdims=True) * mass
        for part in range(4)
    ]
    xx, yy, zz, xy, xz, yz = [m0[row : row + 1] for row in range(6)]
    twice = 2.0 * mass
    out = select_rows(
        [
            sums[1] - x * sums[0],
            sums[2] - y * sums[0],
            sums[3] - z * sums[0],
            twice * (nx * xx + ny * xy + nz * xz),
            twice * (nx * xy + ny * yy + nz * yz),
            twice * (nx * xz + ny * yz + nz * zz),
        ]
    )
    return out, sums[0]


def pair_kernel(
    first_ref, slot_ref, same_ref, count_ref, features_ref, fetched_ref,
    local_ref, returned_ref, energy_ref, left_ref, moment_ref, total_ref,
):
    owned = left_ref.shape[0]
    total_ref[...] = jnp.zeros_like(total_ref)
    returned_ref[...] = jnp.zeros_like(returned_ref)

    def own_rows(block):
        start = pl.multiple_of(block * BLOCK, BLOCK)
        return read_rows(features_ref[:, pl.ds(start, BLOCK)])

    def prepare(block, carry):
        rows = own_rows(block)
        left, _ = exponent_rows(rows)
        left_ref[block] = left_splits(left).T.astype(BF16)
        moment_ref[block] = moment_rows(rows)
        return carry

    lax.fori_loop(0, owned, prepare, 0)

    def visit(entry, carry):
        block = first_ref[entry]
        slot = slot_ref[entry]
        factor = same_ref[entry]
        rows = read_rows(fetched_ref[slot])
        _, right = exponent_rows(rows)
        right = right_splits(right)
        second = moment_rows(rows)
        first = moment_ref[block]
        left = left_ref[block]

        def gaussians(tile):
            columns = slice(tile * TILE, (tile + 1) * TILE)
            value = jnp.exp2(dot(left, right[:, columns], 1, 0))
            high = value.astype(BF16)
            return high, (value - high.astype(F32)).astype(BF16)

        by_first = None
        by_second = []

        def contract(tile, high, low, by_first):
            columns = slice(tile * TILE, (tile + 1) * TILE)
            part = dot(high, second[:, columns], 1, 1) + dot(low, second[:, columns], 1, 1)
            by_first = part if by_first is None else by_first + part
            both = dot(first, high, 1, 0)
            by_second.append(both[0:32] + both[32:64] + dot(first[0:32], low, 1, 0))
            return by_first

        tiles = BLOCK // TILE
        held = gaussians(0)
        for tile in range(tiles):
            later = gaussians(tile + 1) if tile + 1 < tiles else None
            by_first = contract(tile, *held, by_first)
            held = later
        total_ref[block] += factor * by_first
        returned_ref[slot] = finish(rows, jnp.concatenate(by_second, axis=1), factor)[0][0:6]
        return carry

    lax.fori_loop(0, count_ref[0], visit, 0)

    def close(block, energy):
        rows = own_rows(block)
        both = total_ref[block].T
        out, share = finish(rows, both[0:32] + both[32:64], 1.0)
        start = pl.multiple_of(block * BLOCK, BLOCK)
        local_ref[:, pl.ds(start, BLOCK)] = out[0:6]
        return energy + share

    energy = lax.fori_loop(0, owned, close, jnp.zeros((1, BLOCK), F32))
    energy_ref[...] = energy


def shards(features, first_slot, second_owner, second_slot, pair_count):
    owned = features.shape[1] // BLOCK
    blocks = features.reshape(7, owned, BLOCK).transpose(1, 0, 2)
    entries = first_slot.shape[0]
    groups = lax.axis_size("gy")
    capacity = max(2, entries // groups)
    slots = groups * capacity
    self_index = lax.axis_index("gy")
    owners = second_owner[:, 0]
    live = jnp.arange(entries, dtype=jnp.int32) < pair_count[0]
    factors = jnp.where((owners == self_index) & (second_slot == first_slot), 1.0, 2.0).astype(F32)
    owner_hits = (owners[:, None] == jnp.arange(groups, dtype=jnp.int32)[None, :]) & live[:, None]
    running = jnp.cumsum(owner_hits.astype(jnp.int32), axis=0) - 1
    order_rank = jnp.sum(jnp.where(owner_hits, running, 0), axis=1)
    slot_index = owners * capacity + order_rank
    slot_table = (
        slot_index[:, None] == jnp.arange(slots, dtype=jnp.int32)[None, :]
    ) & live[:, None]
    wanted = jnp.sum(jnp.where(slot_table, second_slot[:, None] + 1, 0), axis=0) - 1
    requested = lax.all_to_all(
        wanted.reshape(groups, capacity), "gy", split_axis=0, concat_axis=0, tiled=True
    ).reshape(slots)
    outgoing = blocks[jnp.clip(requested, 0, owned - 1)]
    fetched = lax.all_to_all(
        outgoing.reshape(groups, capacity, 7, BLOCK), "gy", split_axis=0, concat_axis=0, tiled=True
    ).reshape(slots, 7, BLOCK)

    smem = pl.BlockSpec(memory_space=pltpu.SMEM)
    vmem = pl.BlockSpec(memory_space=pltpu.VMEM)
    local_grads, returned, energy_rows = pl.pallas_call(
        pair_kernel,
        out_shape=[
            jax.ShapeDtypeStruct((6, owned * BLOCK), F32),
            jax.ShapeDtypeStruct((slots, 6, BLOCK), F32),
            jax.ShapeDtypeStruct((1, BLOCK), F32),
        ],
        in_specs=[smem, smem, smem, smem, vmem, vmem],
        out_specs=[vmem, vmem, vmem],
        scratch_shapes=[
            pltpu.VMEM((owned, BLOCK, 48), BF16),
            pltpu.VMEM((owned, 64, BLOCK), BF16),
            pltpu.VMEM((owned, BLOCK, 64), F32),
        ],
        compiler_params=pltpu.CompilerParams(vmem_limit_bytes=48 * 2**20),
    )(first_slot, slot_index, factors, pair_count, features, fetched)

    arrived = lax.all_to_all(
        returned.reshape(groups, capacity, 6, BLOCK),
        "gy",
        split_axis=0,
        concat_axis=0,
        tiled=True,
    ).reshape(slots, 6, BLOCK)
    selector = (requested[:, None] == jnp.arange(owned, dtype=jnp.int32)[None, :]).astype(F32)
    remote = jnp.einsum("sl,sfb->flb", selector, arrived, precision=lax.Precision.HIGHEST)
    gradient = local_grads + remote.reshape(6, owned * BLOCK)
    total = lax.psum(jnp.sum(energy_rows), ("gx", "gy"))
    return (gradient, total / BLOCK)


def solution(mesh):
    return jax.shard_map(
        shards,
        mesh=mesh,
        in_specs=(
            P(None, ("gx", "gy")),
            P(("gx", "gy")),
            P(("gx", "gy"), None),
            P(("gx", "gy")),
            P(("gx", "gy")),
        ),
        out_specs=(P(None, ("gx", "gy")), P()),
        check_vma=False,
    )
```

time: 1550 us -> 226 us (0.15); the launches traced: 1530 us -> 225 us
  matrix products: 516 us -> 0.62 us
  starting transfers between devices: 529 us -> 27.1 us
  other arithmetic: 157 us -> 5.18 us
  loops' own time: 134 us -> 0 us
  local copies, waits for them, and re-layouts: 77.4 us -> 10.2 us
  Pallas kernels: 0 us -> 60.9 us
    dot_general x81 -> x1, matrix products: 516 us -> 0.62 us  [shards(): jnp.einsum('sl,sfb->flb', selector, arrived, precision=lax.Precision.HIGH...]
    all_to_all x2, starting transfers between devices: 529 us -> 27.1 us  [the longest x1 22.7 us: shards(): lax.all_to_all(returned.reshape(groups, capacity, 6, BLOCK), 'gy', split_...]
    another operation x1 -> x0, loops' own time: 134 us -> none  [shards(): lax.fori_loop(0, live_count, visit_entry, (local_grads, returned_init, en...]
    reduce_sum x20 -> x1, other arithmetic: 112 us -> 0.61 us  [shards(): total = lax.psum(jnp.sum(energy_rows), ('gx', 'gy'))]
    pallas_call x0 -> x1, Pallas kernels: none -> 60.9 us  [shards(): pl.pallas_call(pair_kernel, out_shape=[jax.ShapeDtypeStruct((6, owned * B...]
    dynamic_slice x60 -> x0, local copies, waits for them, and re-layouts: 35.5 us -> none  [the longest x20 12.4 us: visit_entry(): grads_now = grads_now.at[first_slot[entry_index]].add(grad_first)]
    another operation x40 -> x0, other arithmetic: 28.7 us -> none
    slice x20 -> x0, local copies, waits for them, and re-layouts: 25.1 us -> none  [tile_terms(): weights = first_block[6][:, None] * second_block[6][None, :]]
where the time goes in v1:
time: 226 us; the launch traced here: 225 us
  blocking collectives  93.1 us (41%)
  Pallas kernels  60.9 us (27%)
  starting transfers between devices  27.1 us (12%)
  waiting for transfers between devices  24.9 us (11%)
  local copies, waits for them, and re-layouts  10.2 us (5%)
  other arithmetic  5.18 us (2%)
  between operations  3.24 us (1%)
    psum x1, blocking collectives, shards(): total = lax.psum(jnp.sum(energy_rows), ('gx', 'gy'))  77 us
    pallas_call x1, Pallas kernels, shards(): pl.pallas_call(pair_kernel, out_shape=[jax.ShapeDtypeStruct((6, owned * B...  60.9 us
    all_to_all x1, waiting for transfers between devices, shards(): lax.all_to_all(outgoing.reshape(groups, capacity, 7, BLOCK), 'gy', split_...  24.9 us
    all_to_all x1, starting transfers between devices, shards(): lax.all_to_all(returned.reshape(groups, capacity, 6, BLOCK), 'gy', split_...  22.7 us
    all_to_all x1, blocking collectives, shards(): lax.all_to_all(wanted.reshape(groups, capacity), 'gy', split_axis=0, conc...  16.2 us
  transfers between devices with their start and end apart: 2, of which 1 were waited for; matrix products, arithmetic and copies ran while one was open for 0% of the time, Pallas kernels for 0%

profile of v1, /device:TPU:1, one launch (start us, length us, event | category | flops | bytes accessed | tf_op | source)
XLA Modules:
  0.0 225.3 jit_solution(17361491578541498666)
XLA Ops:
  1.3 0.7 broadcast_add_fusion.1
  1.9 0.7 fusion.1
  2.7 0.1 reduce_window_sum.11
  2.7 0.8 select_reduce_fusion.1
  3.6 0.7 fusion.7
  4.2 0.1 select_reduce_fusion
  4.3 0.1 sub.12
  4.5 16.2 %all_to_all.16 = s32[32,1,2]{2,1,0:T(1,128)S(1)} all-to-all(s32[32,1,2]{2,1,0:T(1,128)S(1)} %bitcast.35), channel_id=1, replica_groups=mesh['gx'=4,'gy'=32] {'gy'}, dimensions={0} | all-to-all | bytes 512 | tf_op jit(solution)/shard_map/all_to_all | solution.py:190
  20.6 0.5 broadcast.69
  21.1 0.7 fusion.8
  21.9 0.1 min.12
  22.0 1.6 gather_fusion
  23.7 2.7 %copy.16 = f32[32,2,7,1024]{3,1,2,0:T(2,128)} copy(f32[32,2,7,1024]{3,2,1,0:T(8,128)S(1)} %bitcast.33) | data formatting | bytes 3670016 | tf_op jit(solution)/shard_map/reshape | solution.py:195
  26.3 0.0 copy-start.2
  26.4 0.0 copy-start.1
  26.4 0.0 copy-start.3
  26.4 4.4 %all-to-all-start.1 = ((f32[32,2,7,1024]{3,1,2,0:T(2,128)}), f32[32,2,7,1024]{3,1,2,0:T(2,128)S(1)}, u32[]{:S(2)}, u32[]{:S(2)}) async-start(f32[32,2,7,1024]{3,1,2,0:T(2,128)} %copy.16), calls=%async_computation.1 | async-start | bytes 3670016 | tf_op jit(solution)/shard_map/all_to_all | solution.py:194
  30.8 0.0 copy-done.2
  30.8 0.0 copy-done.1
  30.8 0.0 copy-done.3
  30.8 0.0 copy-start
  30.9 24.9 %all-to-all-done.1 = f32[32,2,7,1024]{3,1,2,0:T(2,128)S(1)} async-done(((f32[32,2,7,1024]{3,1,2,0:T(2,128)}), f32[32,2,7,1024]{3,1,2,0:T(2,128)S(1)}, u32[]{:S(2)}, u32[]{:S(2)}) %all-to-all-start.1) | async-done | bytes 1835040 | tf_op jit(solution)/shard_map/all_to_all | solution.py:194
  55.8 0.8 copy.17
  56.6 0.0 copy-done
  56.6 60.9 %shard_map.68 = (f32[6,8192]{1,0:T(8,128)S(1)}, f32[64,6,1024]{2,1,0:T(8,128)S(1)}, f32[1,1024]{1,0:T(1,128)S(1)}) custom-call(s32[32]{0:T(128)S(1)} %copy-done.1, s32[32]{0:T(128)S(1)} %multiply_add_fusion.slot_ref, f32[32]{0:T(128)S(1)} %and_select_fusion.same_ref, s32[1]{0:T(128)} %copy.21.count_ref, f32[7,8192]{1,0:T(8,128)S(1)} %copy-done, ...), custom_call_target="tpu_custom_call" | custom-call | tf_op jit(solution)/shard_map/pallas_call | solution.py:200
  117.5 2.4 %copy.18 = f32[32,2,6,1024]{3,1,2,0:T(2,128)} copy(f32[32,2,6,1024]{3,2,1,0:T(8,128)S(1)} %bitcast.32) | data formatting | bytes 3145728 | tf_op jit(solution)/shard_map/reshape | solution.py:218
  119.9 22.7 %all-to-all-start.2 = ((f32[32,2,6,1024]{3,1,2,0:T(2,128)}), f32[32,2,6,1024]{3,1,2,0:T(2,128)S(1)}, u32[]{:S(2)}, u32[]{:S(2)}) async-start(f32[32,2,6,1024]{3,1,2,0:T(2,128)} %copy.18), calls=%async_computation.2 | async-start | bytes 3145728 | tf_op jit(solution)/shard_map/all_to_all | solution.py:217
  142.6 0.6 reduce_sum.32
  143.2 0.1 eq.62
  143.3 77.0 %psum.7 = f32[]{:T(128)} all-reduce(f32[]{:T(128)} %reduce_sum.32), channel_id=1, replica_groups=mesh['gx'=4,'gy'=32] {'gx','gy'}, use_global_device_ids=true, to_apply=%region_4.5 | all-reduce | flops 1 | bytes 8 | tf_op jit(solution)/shard_map/psum | solution.py:227
  220.9 0.0 all-to-all-done.2
  220.9 0.6 copy.19
  221.6 1.1 reshape.75
  222.7 0.6 convolution_bitcast_fusion
  223.3 0.1 copy.20
  223.4 0.7 add.47
  (6 shorter events, 0.0 us)
Async XLA Ops:
  26.3 4.4 %copy-start.2 = (s32[32,1]{0,1:T(1,128)S(1)}, s32[32,1]{0,1:T(1,128)}, u32[]{:S(2)}) copy-start(s32[32,1]{0,1:T(1,128)} %param.7) | copy-start | bytes 388
  26.4 4.5 %copy-start.1 = (s32[32]{0:T(128)S(1)}, s32[32]{0:T(128)}, u32[]{:S(2)}) copy-start(s32[32]{0:T(128)} %first_ref.1) | copy-start | bytes 388
  26.4 4.5 %copy-start.3 = (s32[32]{0:T(128)S(1)}, s32[32]{0:T(128)}, u32[]{:S(2)}) copy-start(s32[32]{0:T(128)} %param.8) | copy-start | bytes 388
  26.4 29.4 %all-to-all-start.1 = ((f32[32,2,7,1024]{3,1,2,0:T(2,128)}), f32[32,2,7,1024]{3,1,2,0:T(2,128)S(1)}, u32[]{:S(2)}, u32[]{:S(2)}) async-start(f32[32,2,7,1024]{3,1,2,0:T(2,128)} %copy.16), calls=%async_computation.1 | async-start | bytes 3670016 | tf_op jit(solution)/shard_map/all_to_all | solution.py:194
  30.8 25.8 %copy-start = (f32[7,8192]{1,0:T(8,128)S(1)}, f32[7,8192]{1,0:T(8,128)}, u32[]{:S(2)}) copy-start(f32[7,8192]{1,0:T(8,128)} %features_ref.1) | copy-start | bytes 688132
  119.9 101.0 %all-to-all-start.2 = ((f32[32,2,6,1024]{3,1,2,0:T(2,128)}), f32[32,2,6,1024]{3,1,2,0:T(2,128)S(1)}, u32[]{:S(2)}, u32[]{:S(2)}) async-start(f32[32,2,6,1024]{3,1,2,0:T(2,128)} %copy.18), calls=%async_computation.2 | async-start | bytes 3145728 | tf_op jit(solution)/shard_map/all_to_all | solution.py:217

commit v2 on v1

v2 whole, which is shorter than its diff:
```python
import jax
import jax.numpy as jnp
from jax import lax
from jax.experimental import pallas as pl
from jax.experimental.pallas import tpu as pltpu
from jax.sharding import PartitionSpec as P

BLOCK = 1024
TILE = 256
LOG2E = 1.4426950408889634
F32 = jnp.float32
BF16 = jnp.bfloat16


def dot(left, right, left_dim, right_dim):
    return lax.dot_general(
        left, right, (((left_dim,), (right_dim,)), ((), ())), preferred_element_type=F32
    )


def split_three(value):
    high = value.astype(BF16).astype(F32)
    rest = value - high
    mid = rest.astype(BF16).astype(F32)
    return high, mid, rest - mid


def select_rows(rows):
    index = lax.broadcasted_iota(jnp.int32, (8, BLOCK), 0)
    tile = jnp.zeros((8, BLOCK), F32)
    for place, row in enumerate(rows):
        tile = jnp.where(index == place, row, tile)
    return tile


def read_rows(block):
    return [block[row : row + 1] for row in range(7)]


def exponent_rows(rows):
    x, y, z = rows[:3]
    norm = (-0.5 * LOG2E) * (x * x + y * y + z * z)
    one = jnp.ones_like(x)
    left = select_rows([LOG2E * x, LOG2E * y, LOG2E * z, one, norm])
    right = select_rows([x, y, z, norm, one])
    return left, right


def left_splits(left):
    high, mid, low = split_three(left)
    return jnp.concatenate([high, high, mid, mid, high, low], axis=0)


def right_splits(right):
    high, mid, low = split_three(right)
    return jnp.concatenate([high, mid, high, mid, low, high], axis=0).astype(BF16)


def normal_products(rows):
    nx, ny, nz = rows[3:6]
    return select_rows([nx, ny, nz, nx, nx, ny]) * select_rows([nx, ny, nz, ny, nz, nz])


def moment_rows(rows):
    x, y, z, w = rows[0], rows[1], rows[2], rows[6]
    base = normal_products(rows) * w
    full = jnp.concatenate([base, base * x, base * y, base * z], axis=0)
    high = full.astype(BF16)
    low = (full - high.astype(F32)).astype(BF16)
    return jnp.concatenate([high, low], axis=0)


def finish(rows, moments, factor):
    x, y, z, nx, ny, nz, w = rows
    index = lax.broadcasted_iota(jnp.int32, (8, BLOCK), 0)
    doubled = normal_products(rows) * jnp.where(index < 3, 1.0, 2.0)
    mass = w * factor
    m0 = moments[0:8]
    sums = [
        jnp.sum(doubled * moments[8 * part : 8 * part + 8], axis=0, keepdims=True) * mass
        for part in range(4)
    ]
    xx, yy, zz, xy, xz, yz = [m0[row : row + 1] for row in range(6)]
    twice = 2.0 * mass
    out = select_rows(
        [
            sums[1] - x * sums[0],
            sums[2] - y * sums[0],
            sums[3] - z * sums[0],
            twice * (nx * xx + ny * xy + nz * xz),
            twice * (nx * xy + ny * yy + nz * yz),
            twice * (nx * xz + ny * yz + nz * zz),
        ]
    )
    return out, sums[0]


def pair_kernel(
    plan_ref, want_ref, features_ref,
    grad_ref, energy_ref,
    block_ref, left_ref, moment_ref, ask_ref, asked_ref, out_ref,
    near_ref, far_ref, twin_ref, now_ref, mine_ref, result_ref, back_ref, home_ref,
    share_ref, across_ref, along_ref, send_sem, recv_sem, local_sem,
):
    groups = want_ref.shape[0]
    rows_x = lax.axis_size("gx")
    owned = block_ref.shape[0]
    near = near_ref.shape[0]
    head = near - groups // 2
    me = lax.axis_index("gy")
    my_row = lax.axis_index("gx")

    def ahead(r):
        return {"gy": lax.rem(me + r, groups)}

    def behind(r):
        return {"gy": lax.rem(me + groups - r, groups)}

    def remote(kind, r, source, target, device):
        return pltpu.make_async_remote_copy(
            src_ref=source, dst_ref=target, send_sem=send_sem.at[kind, r], recv_sem=recv_sem.at[kind, r],
            device_id=device, device_id_type=pl.DeviceIdType.MESH,
        )

    def ask(r):
        return remote(0, r, want_ref.at[r], ask_ref.at[r], ahead(r))

    def fetch_near(r):
        return remote(1, r, out_ref.at[r], near_ref.at[r], behind(r))

    def fetch_far(r):
        return remote(1, r, out_ref.at[r], far_ref.at[r - near], behind(r))

    def fetch_twin(r):
        return remote(2, r, out_ref.at[groups + r], twin_ref.at[r], behind(r))

    def give_back(rank, r):
        return remote(3 + rank, r, back_ref.at[rank * groups + r], home_ref.at[rank * groups + r], ahead(r))

    def share_across(r):
        return remote(5, r, share_ref.at[0], across_ref.at[my_row], {"gx": lax.rem(my_row + r, rows_x)})

    def share_along(r):
        return remote(6, r, share_ref.at[1], along_ref.at[me], ahead(r))

    def arrive_across(r):
        source_row = lax.rem(my_row + rows_x - r, rows_x)
        remote(5, r, share_ref.at[0], across_ref.at[source_row], {"gx": source_row}).wait_recv()

    def arrive_along(r):
        source = lax.rem(me + groups - r, groups)
        remote(6, r, share_ref.at[1], along_ref.at[source], {"gy": source}).wait_recv()

    def each(first, last, body):
        def step(r, carry):
            body(r)
            return carry

        lax.fori_loop(first, last, step, 0)

    barrier = pltpu.get_barrier_semaphore()

    def greet(r):
        pl.semaphore_signal(barrier, inc=1, device_id=ahead(r), device_id_type=pl.DeviceIdType.MESH)

    def greet_across(r):
        pl.semaphore_signal(
            barrier, inc=1, device_id={"gx": lax.rem(my_row + r, rows_x)}, device_id_type=pl.DeviceIdType.MESH
        )

    each(1, groups, greet)
    each(1, rows_x, greet_across)
    for block in range(owned):
        block_ref[block] = features_ref[:, block * BLOCK : (block + 1) * BLOCK]
    pl.semaphore_wait(barrier, groups - 1 + rows_x - 1)

    each(1, groups, lambda r: ask(r).start())
    ask_ref[0] = want_ref[0]
    each(1, groups, lambda r: ask(r).wait_recv())
    fetch_plan = pltpu.make_async_copy(ask_ref, asked_ref, local_sem)
    fetch_plan.start()
    fetch_plan.wait()

    def load_out(place, r):
        out_ref[place * groups + r] = block_ref[jnp.maximum(asked_ref[r, 0, place], 0)]

    def send_near(r):
        load_out(0, r)
        fetch_near(r).start()

    def send_far(r):
        load_out(0, r)
        fetch_far(r).start()

    def send_twin(r):
        load_out(1, r)
        fetch_twin(r).start()

    each(1, near, send_near)
    each(near, groups, send_far)
    each(1, groups, send_twin)
    near_ref[0] = block_ref[jnp.maximum(asked_ref[0, 0, 0], 0)]
    twin_ref[0] = block_ref[jnp.maximum(asked_ref[0, 0, 1], 0)]

    def prepare(block):
        rows = read_rows(block_ref[block])
        left, _ = exponent_rows(rows)
        left_ref[block] = left_splits(left).T.astype(BF16)
        moment_ref[block] = moment_rows(rows)

    each(0, owned, prepare)
    result_ref[groups] = jnp.zeros_like(result_ref[groups])
    each(1, near, lambda r: fetch_near(r).wait_recv())

    def visit(step, energy):
        @pl.when(step == head)
        def _():
            each(near, groups, lambda r: fetch_far(r).wait_recv())

        @pl.when(step == groups // 2)
        def _():
            each(1, groups, lambda r: fetch_twin(r).wait_recv())

        block = plan_ref[step]
        key = plan_ref[groups + step]
        factor = plan_ref[6 * groups + step].astype(F32)
        now_ref[...] = near_ref[jnp.minimum(key, near - 1)]

        @pl.when(step >= head)
        def _():
            far_block = far_ref[jnp.clip(key - near, 0, groups - near - 1)]
            now_ref[...] = jnp.where(key >= near, far_block, now_ref[...])

        @pl.when(step >= groups // 2)
        def _():
            twin_block = twin_ref[jnp.maximum(key - groups, 0)]
            now_ref[...] = jnp.where(key >= groups, twin_block, now_ref[...])

        rows = read_rows(now_ref[...])
        _, right = exponent_rows(rows)
        right = right_splits(right)
        second = moment_rows(rows)
        first = moment_ref[block]
        left = left_ref[block]

        def gaussians(tile):
            columns = slice(tile * TILE, (tile + 1) * TILE)
            value = jnp.exp2(dot(left, right[:, columns], 1, 0))
            high = value.astype(BF16)
            return high, (value - high.astype(F32)).astype(BF16)

        by_first = None
        by_second = []

        def contract(tile, high, low, by_first):
            columns = slice(tile * TILE, (tile + 1) * TILE)
            both = dot(second[:, columns], high, 1, 1)
            part = both[0:32] + both[32:64] + dot(second[0:32, columns], low, 1, 1)
            by_first = part if by_first is None else by_first + part
            both = dot(first, high, 1, 0)
            by_second.append(both[0:32] + both[32:64] + dot(first[0:32], low, 1, 0))
            return by_first

        tiles = BLOCK // TILE
        held = gaussians(0)
        for tile in range(tiles):
            later = gaussians(tile + 1) if tile + 1 < tiles else None
            by_first = contract(tile, *held, by_first)
            held = later
        mine_ref[step] = by_first
        out, share = finish(rows, jnp.concatenate(by_second, axis=1), factor)
        result_ref[step] = out[0:6]
        back_ref[step] = result_ref[plan_ref[2 * groups + step]]

        @pl.when(step >= 1)
        def _():
            give_back(0, step).start()

        return energy + share

    energy = lax.fori_loop(0, groups, visit, jnp.zeros((1, BLOCK), F32))
    share_ref[0] = jnp.full(share_ref.shape[1:], jnp.sum(energy) * (1.0 / BLOCK), F32)
    each(1, rows_x, lambda r: share_across(r).start())

    def send_last(r):
        back_ref[groups + r] = result_ref[plan_ref[3 * groups + r]]
        give_back(1, r).start()

    each(1, groups, send_last)
    back_ref[groups] = result_ref[plan_ref[3 * groups]]
    home_ref[0] = back_ref[0]
    home_ref[groups] = back_ref[groups]

    def close(block):
        def add(step, moments):
            weight = jnp.where(plan_ref[step] == block, plan_ref[6 * groups + step], 0).astype(F32)
            return moments + weight * mine_ref[step]

        moments = lax.fori_loop(0, groups, add, jnp.zeros((32, BLOCK), F32))
        out, _ = finish(read_rows(block_ref[block]), moments, 1.0)
        grad_ref[:, pl.ds(pl.multiple_of(block * BLOCK, BLOCK), BLOCK)] = out[0:6]

    each(0, 1, close)
    across_ref[my_row] = share_ref[0]
    each(1, rows_x, lambda r: share_across(r).wait_send())
    each(1, rows_x, arrive_across)
    total = across_ref[0]
    for r in range(1, rows_x):
        total = total + across_ref[r]
    share_ref[1] = total
    each(1, groups, lambda r: share_along(r).start())
    along_ref[me] = total
    each(1, owned, close)

    each(1, groups, lambda r: give_back(0, r).wait_recv())
    each(1, groups, lambda r: give_back(1, r).wait_recv())

    width = TILE
    for start in range(0, BLOCK, width):
        def gather(slot, sums, start=start):
            piece = home_ref[slot, :, start : start + width]
            wish = asked_ref[lax.rem(slot, groups), 0, slot // groups]
            return tuple(
                kept + jnp.where(wish == block, piece, 0.0) for block, kept in enumerate(sums)
            )

        sums = lax.fori_loop(0, 2 * groups, gather, (jnp.zeros((6, width), F32),) * owned)
        for block in range(owned):
            grad_ref[:, block * BLOCK + start : block * BLOCK + start + width] += sums[block]

    each(1, groups, arrive_along)
    energy_ref[...] = lax.fori_loop(1, groups, lambda r, kept: kept + along_ref[r], along_ref[0])

    def drain(r):
        ask(r).wait_send()
        fetch_twin(r).wait_send()
        give_back(0, r).wait_send()
        give_back(1, r).wait_send()
        share_along(r).wait_send()

    each(1, groups, drain)
    each(1, near, lambda r: fetch_near(r).wait_send())
    each(near, groups, lambda r: fetch_far(r).wait_send())


def shards(features, first_slot, second_owner, second_slot, pair_count):
    owned = features.shape[1] // BLOCK
    entries = first_slot.shape[0]
    groups = lax.axis_size("gy")
    slots = 2 * groups
    near = groups // 2 + groups // 8
    me = lax.axis_index("gy")
    owners = second_owner[:, 0]
    order = jnp.arange(entries, dtype=jnp.int32)
    far = jnp.arange(slots, dtype=jnp.int32)
    live = order < pair_count[0]
    factors = jnp.where((owners == me) & (second_slot == first_slot), 1, 2)
    factors = jnp.where(live, factors, 0)
    rank = jnp.sum((owners[:, None] == owners[None, :]) & (order[None, :] < order[:, None]), axis=1)
    key = rank.astype(jnp.int32) * groups + lax.rem(owners - me + groups, groups)
    place = jnp.sum(key[None, :] < key[:, None], axis=1).astype(jnp.int32)
    at_step = place[None, :] == order[:, None]
    at_slot = key[None, :] == far[:, None]

    def pick(table, values):
        return jnp.sum(jnp.where(table, values[None, :], 0), axis=1)

    want = pick(at_slot, second_slot + 1) - 1
    serve = pick(at_slot, place - groups) + groups
    plan = jnp.concatenate(
        [pick(at_step, first_slot), pick(at_step, key), serve, want, pick(at_step, factors)]
    ).astype(jnp.int32)
    lane = jnp.arange(128, dtype=jnp.int32)[None, :]
    asked = jnp.where(lane == 0, want[:groups, None], jnp.where(lane == 1, want[groups:, None], 0))

    smem = pl.BlockSpec(memory_space=pltpu.SMEM)
    vmem = pl.BlockSpec(memory_space=pltpu.VMEM)
    gradient, energy = pl.pallas_call(
        pair_kernel,
        out_shape=[
            jax.ShapeDtypeStruct((6, owned * BLOCK), F32),
            jax.ShapeDtypeStruct((8, 128), F32),
        ],
        in_specs=[smem, vmem, vmem],
        out_specs=[vmem, vmem],
        scratch_shapes=[
            pltpu.VMEM((owned, 7, BLOCK), F32),
            pltpu.VMEM((owned, BLOCK, 48), BF16),
            pltpu.VMEM((owned, 64, BLOCK), BF16),
            pltpu.VMEM((groups, 1, 128), jnp.int32),
            pltpu.SMEM((groups, 1, 128), jnp.int32),
            pltpu.VMEM((slots, 7, BLOCK), F32),
            pltpu.VMEM((near, 7, BLOCK), F32),
            pltpu.VMEM((groups - near, 7, BLOCK), F32),
            pltpu.VMEM((groups, 7, BLOCK), F32),
            pltpu.VMEM((7, BLOCK), F32),
            pltpu.VMEM((groups, 32, BLOCK), F32),
            pltpu.VMEM((groups + 1, 6, BLOCK), F32),
            pltpu.VMEM((slots, 6, BLOCK), F32),
            pltpu.VMEM((slots, 6, BLOCK), F32),
            pltpu.VMEM((2, 8, 128), F32),
            pltpu.VMEM((lax.axis_size("gx"), 8, 128), F32),
            pltpu.VMEM((groups, 8, 128), F32),
            pltpu.SemaphoreType.DMA((7, groups)),
            pltpu.SemaphoreType.DMA((7, groups)),
            pltpu.SemaphoreType.DMA,
        ],
        compiler_params=pltpu.CompilerParams(
            vmem_limit_bytes=56 * 2**20, collective_id=0, has_side_effects=True
        ),
    )(plan, asked.reshape(groups, 1, 128), features)
    return (gradient, energy[0, 0])


def solution(mesh):
    return jax.shard_map(
        shards,
        mesh=mesh,
        in_specs=(
            P(None, ("gx", "gy")),
            P(("gx", "gy")),
            P(("gx", "gy"), None),
            P(("gx", "gy")),
            P(("gx", "gy")),
        ),
        out_specs=(P(None, ("gx", "gy")), P()),
        check_vma=False,
    )
```

time: 226 us -> 141 us (0.62)
  blocking collectives: 93.1 us -> 0 us
  Pallas kernels: 60.9 us -> 133 us
  starting transfers between devices: 27.1 us -> 0 us
  waiting for transfers between devices: 24.9 us -> 0 us
  local copies, waits for them, and re-layouts: 10.2 us -> 4.89 us
  other arithmetic: 5.18 us -> 1.38 us
    psum x1 -> x0, blocking collectives: 77 us -> none  [shards(): total = lax.psum(jnp.sum(energy_rows), ('gx', 'gy'))]
    pallas_call x1, Pallas kernels: 60.9 us -> 133 us  [shards(): pl.pallas_call(pair_kernel, out_shape=[jax.ShapeDtypeStruct((6, owned * B...]
    all_to_all x2 -> x0, starting transfers between devices: 27.1 us -> none  [the longest x1 22.7 us: shards(): lax.all_to_all(returned.reshape(groups, capacity, 6, BLOCK), 'gy', split_...]
    all_to_all x2 -> x0, waiting for transfers between devices: 24.9 us -> none  [the longest x1 24.9 us: shards(): lax.all_to_all(outgoing.reshape(groups, capacity, 7, BLOCK), 'gy', split_...]
    all_to_all x1 -> x0, blocking collectives: 16.2 us -> none  [shards(): lax.all_to_all(wanted.reshape(groups, capacity), 'gy', split_axis=0, conc...]
    reshape x3 -> x0, local copies, waits for them, and re-layouts: 6.17 us -> none  [the longest x1 2.69 us: shards(): outgoing.reshape(groups, capacity, 7, BLOCK)]
    unnamed x9 -> x7, local copies, waits for them, and re-layouts: 0.14 us -> 2.96 us
  transfers between devices with their start and end apart: 2 -> 0, of which waited for: 1 -> 0; matrix products, arithmetic and copies ran while one was open for 0% -> 0% of each run, Pallas kernels for 0% -> 0%
where the time goes in v2:
time: 141 us
  Pallas kernels  133 us (94%)
  local copies, waits for them, and re-layouts  4.89 us (3%)
    pallas_call x1, Pallas kernels, shards(): pl.pallas_call(pair_kernel, out_shape=[jax.ShapeDtypeStruct((6, owned * B...  133 us
    unnamed x7, local copies, waits for them, and re-layouts  2.96 us

profile of v2, /device:TPU:1, one launch (start us, length us, event | category | flops | bytes accessed | tf_op | source)
XLA Modules:
  0.0 140.9 jit_solution(11627888410602955127)
XLA Ops:
  1.3 0.0 copy-start.1
  1.3 0.6 copy-done.1
  1.9 0.2 convert_reduce_fusion.1
  2.1 0.0 copy-start
  2.1 0.0 copy-start.2
  2.1 0.6 copy-done
  2.8 0.0 copy-done.2
  2.8 0.2 convert_reduce_fusion
  3.0 0.1 select_reduce_fusion.1
  3.1 0.1 select_reduce_fusion
  3.2 0.7 concatenate.3.plan_ref
  3.9 0.1 fusion.6
  4.0 0.7 broadcast_select_fusion.1.want_ref
  4.7 133.3 %shard_map.68 = (f32[6,8192]{1,0:T(8,128)}, f32[8,128]{1,0:T(8,128)}) custom-call(s32[224]{0:T(256)} %concatenate.3.plan_ref, s32[32,1,128]{2,1,0:T(1,128)} %broadcast_select_fusion.1.want_ref, f32[7,8192]{1,0:T(8,128)} %features_ref.1), custom_call_target="tpu_custom_call" | custom-call | tf_op jit(solution)/shard_map/pallas_call | solution.py:378
  138.0 1.2 slice.11
  139.2 1.7 %copy.9 = f32[6,8192]{1,0:T(8,128)} copy(f32[6,8192]{1,0:T(8,128)} %get-tuple-element.22) | data formatting | bytes 393216
  (5 shorter events, 0.0 us)
Async XLA Ops:
  1.3 0.7 copy-start.1
  2.1 0.7 copy-start
  2.1 0.7 copy-start.2

commit v3 on v2

--- a/solution.py
+++ b/solution.py
@@ -110,46 +110,57 @@
     me = lax.axis_index("gy")
     my_row = lax.axis_index("gx")
 
+    def offset(r):
+        half, odd = (r + 1) // 2, lax.rem(r, 2)
+        return odd * half + (1 - odd) * (groups - half)
+
     def ahead(r):
-        return {"gy": lax.rem(me + r, groups)}
+        return {"gy": lax.rem(me + offset(r), groups)}
 
     def behind(r):
-        return {"gy": lax.rem(me + groups - r, groups)}
-
-    def remote(kind, r, source, target, device):
+        return {"gy": lax.rem(me + 2 * groups - offset(r), groups)}
+
+    def remote(kind, source, target, device):
         return pltpu.make_async_remote_copy(
-            src_ref=source, dst_ref=target, send_sem=send_sem.at[kind, r], recv_sem=recv_sem.at[kind, r],
+            src_ref=source, dst_ref=target, send_sem=send_sem.at[kind], recv_sem=recv_sem.at[kind],
             device_id=device, device_id_type=pl.DeviceIdType.MESH,
         )
 
+    def all_of(kind, source, target):
+        return remote(kind, source, target, ahead(1))
+
     def ask(r):
-        return remote(0, r, want_ref.at[r], ask_ref.at[r], ahead(r))
+        return remote(0, want_ref.at[r], ask_ref.at[r], ahead(r))
 
     def fetch_near(r):
-        return remote(1, r, out_ref.at[r], near_ref.at[r], behind(r))
+        return remote(1, out_ref.at[r], near_ref.at[r], behind(r))
 
     def fetch_far(r):
-        return remote(1, r, out_ref.at[r], far_ref.at[r - near], behind(r))
+        return remote(2, out_ref.at[r], far_ref.at[r - near], behind(r))
 
     def fetch_twin(r):
-        return remote(2, r, out_ref.at[groups + r], twin_ref.at[r], behind(r))
+        return remote(3, out_ref.at[groups + r], twin_ref.at[r], behind(r))
 
     def give_back(rank, r):
-        return remote(3 + rank, r, back_ref.at[rank * groups + r], home_ref.at[rank * groups + r], ahead(r))
+        return remote(4 + rank, back_ref.at[rank * groups + r], home_ref.at[rank * groups + r], ahead(r))
 
     def share_across(r):
-        return remote(5, r, share_ref.at[0], across_ref.at[my_row], {"gx": lax.rem(my_row + r, rows_x)})
+        return remote(6, share_ref.at[0], across_ref.at[my_row], {"gx": lax.rem(my_row + r, rows_x)})
 
     def share_along(r):
-        return remote(6, r, share_ref.at[1], along_ref.at[me], ahead(r))
-
-    def arrive_across(r):
-        source_row = lax.rem(my_row + rows_x - r, rows_x)
-        remote(5, r, share_ref.at[0], across_ref.at[source_row], {"gx": source_row}).wait_recv()
-
-    def arrive_along(r):
-        source = lax.rem(me + groups - r, groups)
-        remote(6, r, share_ref.at[1], along_ref.at[source], {"gy": source}).wait_recv()
+        return remote(7, share_ref.at[1], along_ref.at[me], ahead(r))
+
+    others = pl.ds(1, groups - 1)
+    twins = pl.ds(groups + 1, groups - 1)
+    all_asks = all_of(0, want_ref.at[others], ask_ref.at[others])
+    all_near = all_of(1, out_ref.at[pl.ds(1, near - 1)], near_ref.at[pl.ds(1, near - 1)])
+    all_far = all_of(2, out_ref.at[pl.ds(near, groups - near)], far_ref)
+    all_twin = all_of(3, out_ref.at[twins], twin_ref.at[others])
+    all_first = all_of(4, back_ref.at[others], home_ref.at[others])
+    all_last = all_of(5, back_ref.at[twins], home_ref.at[twins])
+    rest_x = pl.ds(0, rows_x - 1)
+    all_across = all_of(6, across_ref.at[rest_x], across_ref.at[rest_x])
+    all_along = all_of(7, along_ref.at[others], along_ref.at[others])
 
     def each(first, last, body):
         def step(r, carry):
@@ -176,7 +187,7 @@
 
     each(1, groups, lambda r: ask(r).start())
     ask_ref[0] = want_ref[0]
-    each(1, groups, lambda r: ask(r).wait_recv())
+    all_asks.wait_recv()
     fetch_plan = pltpu.make_async_copy(ask_ref, asked_ref, local_sem)
     fetch_plan.start()
     fetch_plan.wait()
@@ -210,16 +221,16 @@
 
     each(0, owned, prepare)
     result_ref[groups] = jnp.zeros_like(result_ref[groups])
-    each(1, near, lambda r: fetch_near(r).wait_recv())
+    all_near.wait_recv()
 
     def visit(step, energy):
         @pl.when(step == head)
         def _():
-            each(near, groups, lambda r: fetch_far(r).wait_recv())
+            all_far.wait_recv()
 
         @pl.when(step == groups // 2)
         def _():
-            each(1, groups, lambda r: fetch_twin(r).wait_recv())
+            all_twin.wait_recv()
 
         block = plan_ref[step]
         key = plan_ref[groups + step]
@@ -302,8 +313,7 @@
 
     each(0, 1, close)
     across_ref[my_row] = share_ref[0]
-    each(1, rows_x, lambda r: share_across(r).wait_send())
-    each(1, rows_x, arrive_across)
+    all_across.wait_recv()
     total = across_ref[0]
     for r in range(1, rows_x):
         total = total + across_ref[r]
@@ -312,35 +322,27 @@
     along_ref[me] = total
     each(1, owned, close)
 
-    each(1, groups, lambda r: give_back(0, r).wait_recv())
-    each(1, groups, lambda r: give_back(1, r).wait_recv())
-
-    width = TILE
-    for start in range(0, BLOCK, width):
-        def gather(slot, sums, start=start):
-            piece = home_ref[slot, :, start : start + width]
-            wish = asked_ref[lax.rem(slot, groups), 0, slot // groups]
-            return tuple(
-                kept + jnp.where(wish == block, piece, 0.0) for block, kept in enumerate(sums)
-            )
-
-        sums = lax.fori_loop(0, 2 * groups, gather, (jnp.zeros((6, width), F32),) * owned)
-        for block in range(owned):
-            grad_ref[:, block * BLOCK + start : block * BLOCK + start + width] += sums[block]
-
-    each(1, groups, arrive_along)
-    energy_ref[...] = lax.fori_loop(1, groups, lambda r, kept: kept + along_ref[r], along_ref[0])
-
-    def drain(r):
-        ask(r).wait_send()
-        fetch_twin(r).wait_send()
-        give_back(0, r).wait_send()
-        give_back(1, r).wait_send()
-        share_along(r).wait_send()
-
-    each(1, groups, drain)
-    each(1, near, lambda r: fetch_near(r).wait_send())
-    each(near, groups, lambda r: fetch_far(r).wait_send())
+    def gather(first, last):
+        for start in range(0, BLOCK, TILE):
+
+            def add(slot, sums, start=start):
+                piece = home_ref[slot, :, start : start + TILE]
+                wish = asked_ref[lax.rem(slot, groups), 0, slot // groups]
+                return tuple(kept + jnp.where(wish == block, piece, 0.0) for block, kept in enumerate(sums))
+
+            sums = lax.fori_loop(first, last, add, (jnp.zeros((6, TILE), F32),) * owned)
+            for block in range(owned):
+                grad_ref[:, block * BLOCK + start : block * BLOCK + start + TILE] += sums[block]
+
+    all_first.wait_recv()
+    gather(0, groups)
+    all_along.wait_recv()
+    total = lax.fori_loop(1, groups, lambda r, kept: kept + along_ref[r], along_ref[0])
+    energy_ref[0, 0] = jnp.max(total)
+    all_last.wait_recv()
+    gather(groups, 2 * groups)
+    for copies in (all_asks, all_near, all_far, all_twin, all_first, all_last, all_across, all_along):
+        copies.wait_send()
 
 
 def shards(features, first_slot, second_owner, second_slot, pair_count):
@@ -357,7 +359,9 @@
     factors = jnp.where((owners == me) & (second_slot == first_slot), 1, 2)
     factors = jnp.where(live, factors, 0)
     rank = jnp.sum((owners[:, None] == owners[None, :]) & (order[None, :] < order[:, None]), axis=1)
-    key = rank.astype(jnp.int32) * groups + lax.rem(owners - me + groups, groups)
+    ahead = lax.rem(owners - me + groups, groups)
+    distance = jnp.where(ahead <= groups // 2, jnp.maximum(2 * ahead - 1, 0), 2 * (groups - ahead))
+    key = rank.astype(jnp.int32) * groups + distance
     place = jnp.sum(key[None, :] < key[:, None], axis=1).astype(jnp.int32)
     at_step = place[None, :] == order[:, None]
     at_slot = key[None, :] == far[:, None]
@@ -379,10 +383,10 @@
         pair_kernel,
         out_shape=[
             jax.ShapeDtypeStruct((6, owned * BLOCK), F32),
-            jax.ShapeDtypeStruct((8, 128), F32),
+            jax.ShapeDtypeStruct((1, 1), F32),
         ],
         in_specs=[smem, vmem, vmem],
-        out_specs=[vmem, vmem],
+        out_specs=[vmem, smem],
         scratch_shapes=[
             pltpu.VMEM((owned, 7, BLOCK), F32),
             pltpu.VMEM((owned, BLOCK, 48), BF16),
@@ -401,15 +405,15 @@
             pltpu.VMEM((2, 8, 128), F32),
             pltpu.VMEM((lax.axis_size("gx"), 8, 128), F32),
             pltpu.VMEM((groups, 8, 128), F32),
-            pltpu.SemaphoreType.DMA((7, groups)),
-            pltpu.SemaphoreType.DMA((7, groups)),
+            pltpu.SemaphoreType.DMA((8,)),
+            pltpu.SemaphoreType.DMA((8,)),
             pltpu.SemaphoreType.DMA,
         ],
         compiler_params=pltpu.CompilerParams(
             vmem_limit_bytes=56 * 2**20, collective_id=0, has_side_effects=True
         ),
     )(plan, asked.reshape(groups, 1, 128), features)
-    return (gradient, energy[0, 0])
+    return (gradient, energy.reshape(()))
 
 
 def solution(mesh):

time: 141 us -> 132 us (0.936)
  Pallas kernels: 133 us -> 123 us
  between operations: 1.33 us -> 3.1 us
    pallas_call x1, Pallas kernels: 133 us -> 123 us  [shards(): pl.pallas_call(pair_kernel, out_shape=[jax.ShapeDtypeStruct((6, owned * B...]
where the time goes in v3:
time: 132 us; the launch traced here: 131 us
  Pallas kernels  123 us (93%)
  local copies, waits for them, and re-layouts  3.69 us (3%)
  between operations  3.1 us (2%)
  other arithmetic  1.39 us (1%)
    pallas_call x1, Pallas kernels, shards(): pl.pallas_call(pair_kernel, out_shape=[jax.ShapeDtypeStruct((6, owned * B...  123 us
    unnamed x7, local copies, waits for them, and re-layouts  2.96 us

profile of v3, /device:TPU:1, one launch (start us, length us, event | category | flops | bytes accessed | tf_op | source)
XLA Modules:
  0.0 131.1 jit_solution(14072659852026762904)
XLA Ops:
  1.3 0.0 copy-start.1
  1.3 0.6 copy-done.1
  1.9 0.2 convert_reduce_fusion.1
  2.1 0.0 copy-start
  2.1 0.0 copy-start.2
  2.2 0.6 copy-done
  2.8 0.0 copy-done.2
  2.8 0.2 convert_reduce_fusion
  3.0 0.1 select_reduce_fusion.1
  3.1 0.1 select_reduce_fusion
  3.3 0.7 concatenate.3.plan_ref
  3.9 0.1 fusion.6
  4.0 0.7 broadcast_select_fusion.1.want_ref
  4.7 122.9 %shard_map.68 = (f32[6,8192]{1,0:T(8,128)}, f32[1,1]{1,0:T(1,128)}) custom-call(s32[224]{0:T(256)} %concatenate.3.plan_ref, s32[32,1,128]{2,1,0:T(1,128)} %broadcast_select_fusion.1.want_ref, f32[7,8192]{1,0:T(8,128)} %features_ref.1), custom_call_target="tpu_custom_call" | custom-call | tf_op jit(solution)/shard_map/pallas_call | solution.py:382
  127.6 1.7 %copy.10 = f32[6,8192]{1,0:T(8,128)} copy(f32[6,8192]{1,0:T(8,128)} %get-tuple-element.22) | data formatting | bytes 393216
  (5 shorter events, 0.0 us)
Async XLA Ops:
  1.3 0.7 copy-start.1
  2.1 0.7 copy-start
  2.1 0.7 copy-start.2

commit v4 on v3

--- a/solution.py
+++ b/solution.py
@@ -7,6 +7,7 @@
 
 BLOCK = 1024
 TILE = 256
+DEPTH = 3
 LOG2E = 1.4426950408889634
 F32 = jnp.float32
 BF16 = jnp.bfloat16
@@ -100,7 +101,8 @@
     grad_ref, energy_ref,
     block_ref, left_ref, moment_ref, ask_ref, asked_ref, out_ref,
     near_ref, far_ref, twin_ref, now_ref, mine_ref, result_ref, back_ref, home_ref,
-    share_ref, across_ref, along_ref, send_sem, recv_sem, local_sem,
+    share_ref, across_ref, along_ref, past_ref, high_ref, low_ref, column_ref, partial_ref,
+    send_sem, recv_sem, local_sem,
 ):
     groups = want_ref.shape[0]
     rows_x = lax.axis_size("gx")
@@ -223,7 +225,38 @@
     result_ref[groups] = jnp.zeros_like(result_ref[groups])
     all_near.wait_recv()
 
+    tiles = BLOCK // TILE
+    chunks = tiles * tiles
+
+    def cut(index):
+        return slice(index * TILE, (index + 1) * TILE)
+
+    def first_terms(second, high, low):
+        both = dot(second, high, 1, 1)
+        return both[0:32] + both[32:64] + dot(second[0:32], low, 1, 1)
+
+    def second_terms(first, high, low):
+        both = dot(first, high, 1, 0)
+        return both[0:32] + both[32:64] + dot(first[0:32], low, 1, 0)
+
+    def settle(entry, number, last_column):
+        place = number + DEPTH
+        high, low = high_ref[cut(place)], low_ref[cut(place)]
+        rows = cut(tiles + number)
+        mine_ref[entry, :, rows] += first_terms(column_ref[...], high, low)
+        first = moment_ref[plan_ref[entry], :, rows]
+        return last_column + second_terms(first, high, low)
+
+    def conclude(entry, last_column):
+        moments = jnp.concatenate([partial_ref[:, : BLOCK - TILE], last_column], axis=1)
+        factor = plan_ref[6 * groups + entry].astype(F32)
+        out, share = finish(read_rows(past_ref[...]), moments, factor)
+        result_ref[entry] = out[0:6]
+        return share
+
     def visit(step, energy):
+        past_ref[...] = now_ref[...]
+
         @pl.when(step == head)
         def _():
             all_far.wait_recv()
@@ -234,7 +267,6 @@
 
         block = plan_ref[step]
         key = plan_ref[groups + step]
-        factor = plan_ref[6 * groups + step].astype(F32)
         now_ref[...] = near_ref[jnp.minimum(key, near - 1)]
 
         @pl.when(step >= head)
@@ -247,49 +279,59 @@
             twin_block = twin_ref[jnp.maximum(key - groups, 0)]
             now_ref[...] = jnp.where(key >= groups, twin_block, now_ref[...])
 
+        before = jnp.maximum(step - 1, 0)
         rows = read_rows(now_ref[...])
         _, right = exponent_rows(rows)
         right = right_splits(right)
         second = moment_rows(rows)
         first = moment_ref[block]
         left = left_ref[block]
-
-        def gaussians(tile):
-            columns = slice(tile * TILE, (tile + 1) * TILE)
-            value = jnp.exp2(dot(left, right[:, columns], 1, 0))
+        last_column = partial_ref[:, BLOCK - TILE :]
+        by_first = [None] * tiles
+        by_second = [None] * tiles
+        flying = {}
+
+        def add(sums, index, term):
+            sums[index] = term if sums[index] is None else sums[index] + term
+
+        for chunk in range(chunks):
+            column, row = divmod(chunk, tiles)
+            value = jnp.exp2(dot(left[cut(row)], right[:, cut(column)], 1, 0))
             high = value.astype(BF16)
-            return high, (value - high.astype(F32)).astype(BF16)
-
-        by_first = None
-        by_second = []
-
-        def contract(tile, high, low, by_first):
-            columns = slice(tile * TILE, (tile + 1) * TILE)
-            both = dot(second[:, columns], high, 1, 1)
-            part = both[0:32] + both[32:64] + dot(second[0:32, columns], low, 1, 1)
-            by_first = part if by_first is None else by_first + part
-            both = dot(first, high, 1, 0)
-            by_second.append(both[0:32] + both[32:64] + dot(first[0:32], low, 1, 0))
-            return by_first
-
-        tiles = BLOCK // TILE
-        held = gaussians(0)
-        for tile in range(tiles):
-            later = gaussians(tile + 1) if tile + 1 < tiles else None
-            by_first = contract(tile, *held, by_first)
-            held = later
-        mine_ref[step] = by_first
-        out, share = finish(rows, jnp.concatenate(by_second, axis=1), factor)
-        result_ref[step] = out[0:6]
-        back_ref[step] = result_ref[plan_ref[2 * groups + step]]
-
-        @pl.when(step >= 1)
+            flying[chunk] = high, (value - high.astype(F32)).astype(BF16)
+            if chunk < DEPTH:
+                last_column = settle(before, chunk - DEPTH, last_column)
+            if chunk == DEPTH - 1:
+                energy = energy + conclude(before, last_column)
+            if chunk >= DEPTH:
+                column, row = divmod(chunk - DEPTH, tiles)
+                high, low = flying.pop(chunk - DEPTH)
+                add(by_first, row, first_terms(second[:, cut(column)], high, low))
+                add(by_second, column, second_terms(first[:, cut(row)], high, low))
+        for place in range(DEPTH):
+            high_ref[cut(place)], low_ref[cut(place)] = flying[chunks - DEPTH + place]
+        column_ref[...] = second[:, BLOCK - TILE :]
+        partial_ref[...] = jnp.concatenate(by_second, axis=1)
+        mine_ref[step] = jnp.concatenate(by_first, axis=1)
+        back_ref[before] = result_ref[plan_ref[2 * groups + before]]
+
+        @pl.when(step >= 2)
         def _():
-            give_back(0, step).start()
-
-        return energy + share
-
+            give_back(0, step - 1).start()
+
+        return energy
+
+    for held in (now_ref, high_ref, low_ref, column_ref, partial_ref):
+        held[...] = jnp.zeros_like(held)
+    mine_ref[0] = jnp.zeros_like(mine_ref[0])
     energy = lax.fori_loop(0, groups, visit, jnp.zeros((1, BLOCK), F32))
+    past_ref[...] = now_ref[...]
+    last_column = partial_ref[:, BLOCK - TILE :]
+    for number in range(-DEPTH, 0):
+        last_column = settle(groups - 1, number, last_column)
+    energy = energy + conclude(groups - 1, last_column)
+    back_ref[groups - 1] = result_ref[plan_ref[3 * groups - 1]]
+    give_back(0, groups - 1).start()
     share_ref[0] = jnp.full(share_ref.shape[1:], jnp.sum(energy) * (1.0 / BLOCK), F32)
     each(1, rows_x, lambda r: share_across(r).start())
 
@@ -350,7 +392,7 @@
     entries = first_slot.shape[0]
     groups = lax.axis_size("gy")
     slots = 2 * groups
-    near = groups // 2 + groups // 8
+    near = groups // 2 + max(1, groups // 16)
     me = lax.axis_index("gy")
     owners = second_owner[:, 0]
     order = jnp.arange(entries, dtype=jnp.int32)
@@ -405,6 +447,11 @@
             pltpu.VMEM((2, 8, 128), F32),
             pltpu.VMEM((lax.axis_size("gx"), 8, 128), F32),
             pltpu.VMEM((groups, 8, 128), F32),
+            pltpu.VMEM((7, BLOCK), F32),
+            pltpu.VMEM((DEPTH * TILE, TILE), BF16),
+            pltpu.VMEM((DEPTH * TILE, TILE), BF16),
+            pltpu.VMEM((64, TILE), BF16),
+            pltpu.VMEM((32, BLOCK), F32),
             pltpu.SemaphoreType.DMA((8,)),
             pltpu.SemaphoreType.DMA((8,)),
             pltpu.SemaphoreType.DMA,

time: 132 us -> 122 us (0.924)
  Pallas kernels: 123 us -> 113 us
    pallas_call x1, Pallas kernels: 123 us -> 113 us  [shards(): pl.pallas_call(pair_kernel, out_shape=[jax.ShapeDtypeStruct((6, owned * B...]
where the time goes in v4:
time: 122 us; the launch traced here: 121 us
  Pallas kernels  113 us (93%)
  local copies, waits for them, and re-layouts  3.69 us (3%)
  between operations  3.1 us (3%)
  other arithmetic  1.39 us (1%)
    pallas_call x1, Pallas kernels, shards(): pl.pallas_call(pair_kernel, out_shape=[jax.ShapeDtypeStruct((6, owned * B...  113 us
    unnamed x7, local copies, waits for them, and re-layouts  2.96 us

profile of v4, /device:TPU:1, one launch (start us, length us, event | category | flops | bytes accessed | tf_op | source)
XLA Modules:
  0.0 121.5 jit_solution(979365622809049640)
XLA Ops:
  1.3 0.0 copy-start.1
  1.3 0.6 copy-done.1
  1.9 0.2 convert_reduce_fusion.1
  2.1 0.0 copy-start
  2.1 0.0 copy-start.2
  2.2 0.6 copy-done
  2.8 0.0 copy-done.2
  2.8 0.2 convert_reduce_fusion
  3.0 0.1 select_reduce_fusion.1
  3.1 0.1 select_reduce_fusion
  3.3 0.7 concatenate.3.plan_ref
  3.9 0.1 fusion.6
  4.0 0.7 broadcast_select_fusion.1.want_ref
  4.7 113.3 %shard_map.68 = (f32[6,8192]{1,0:T(8,128)}, f32[1,1]{1,0:T(1,128)}) custom-call(s32[224]{0:T(256)} %concatenate.3.plan_ref, s32[32,1,128]{2,1,0:T(1,128)} %broadcast_select_fusion.1.want_ref, f32[7,8192]{1,0:T(8,128)} %features_ref.1), custom_call_target="tpu_custom_call" | custom-call | tf_op jit(solution)/shard_map/pallas_call | solution.py:424
  118.0 1.7 %copy.10 = f32[6,8192]{1,0:T(8,128)} copy(f32[6,8192]{1,0:T(8,128)} %get-tuple-element.22) | data formatting | bytes 393216
  (5 shorter events, 0.0 us)
Async XLA Ops:
  1.3 0.7 copy-start.1
  2.1 0.7 copy-start
  2.1 0.7 copy-start.2

commit v5 on v4

--- a/solution.py
+++ b/solution.py
@@ -101,7 +101,7 @@
     grad_ref, energy_ref,
     block_ref, left_ref, moment_ref, ask_ref, asked_ref, out_ref,
     near_ref, far_ref, twin_ref, now_ref, mine_ref, result_ref, back_ref, home_ref,
-    share_ref, across_ref, along_ref, past_ref, high_ref, low_ref, column_ref, partial_ref,
+    share_ref, across_ref, along_ref, past_ref, high_ref, low_ref, column_ref, partial_ref, local_ref,
     send_sem, recv_sem, local_sem,
 ):
     groups = want_ref.shape[0]
@@ -243,7 +243,7 @@
         place = number + DEPTH
         high, low = high_ref[cut(place)], low_ref[cut(place)]
         rows = cut(tiles + number)
-        mine_ref[entry, :, rows] += first_terms(column_ref[...], high, low)
+        mine_ref[:, rows] += first_terms(column_ref[...], high, low)
         first = moment_ref[plan_ref[entry], :, rows]
         return last_column + second_terms(first, high, low)
 
@@ -252,6 +252,10 @@
         factor = plan_ref[6 * groups + entry].astype(F32)
         out, share = finish(read_rows(past_ref[...]), moments, factor)
         result_ref[entry] = out[0:6]
+        block = plan_ref[entry]
+        out, _ = finish(read_rows(block_ref[block]), mine_ref[...], factor)
+        for own in range(owned):
+            local_ref[own] += jnp.where(block == own, out, 0.0)
         return share
 
     def visit(step, energy):
@@ -312,7 +316,7 @@
             high_ref[cut(place)], low_ref[cut(place)] = flying[chunks - DEPTH + place]
         column_ref[...] = second[:, BLOCK - TILE :]
         partial_ref[...] = jnp.concatenate(by_second, axis=1)
-        mine_ref[step] = jnp.concatenate(by_first, axis=1)
+        mine_ref[...] = jnp.concatenate(by_first, axis=1)
         back_ref[before] = result_ref[plan_ref[2 * groups + before]]
 
         @pl.when(step >= 2)
@@ -321,9 +325,8 @@
 
         return energy
 
-    for held in (now_ref, high_ref, low_ref, column_ref, partial_ref):
+    for held in (now_ref, high_ref, low_ref, column_ref, partial_ref, mine_ref, local_ref):
         held[...] = jnp.zeros_like(held)
-    mine_ref[0] = jnp.zeros_like(mine_ref[0])
     energy = lax.fori_loop(0, groups, visit, jnp.zeros((1, BLOCK), F32))
     past_ref[...] = now_ref[...]
     last_column = partial_ref[:, BLOCK - TILE :]
@@ -339,32 +342,21 @@
         back_ref[groups + r] = result_ref[plan_ref[3 * groups + r]]
         give_back(1, r).start()
 
-    each(1, groups, send_last)
-    back_ref[groups] = result_ref[plan_ref[3 * groups]]
-    home_ref[0] = back_ref[0]
-    home_ref[groups] = back_ref[groups]
-
-    def close(block):
-        def add(step, moments):
-            weight = jnp.where(plan_ref[step] == block, plan_ref[6 * groups + step], 0).astype(F32)
-            return moments + weight * mine_ref[step]
-
-        moments = lax.fori_loop(0, groups, add, jnp.zeros((32, BLOCK), F32))
-        out, _ = finish(read_rows(block_ref[block]), moments, 1.0)
-        grad_ref[:, pl.ds(pl.multiple_of(block * BLOCK, BLOCK), BLOCK)] = out[0:6]
-
-    each(0, 1, close)
+    each(1, groups // 2, send_last)
+    all_across.wait_recv()
     across_ref[my_row] = share_ref[0]
-    all_across.wait_recv()
     total = across_ref[0]
     for r in range(1, rows_x):
         total = total + across_ref[r]
     share_ref[1] = total
     each(1, groups, lambda r: share_along(r).start())
     along_ref[me] = total
-    each(1, owned, close)
-
-    def gather(first, last):
+    each(groups // 2, groups, send_last)
+    back_ref[groups] = result_ref[plan_ref[3 * groups]]
+    home_ref[0] = back_ref[0]
+    home_ref[groups] = back_ref[groups]
+
+    def gather(first, last, into):
         for start in range(0, BLOCK, TILE):
 
             def add(slot, sums, start=start):
@@ -374,15 +366,16 @@
 
             sums = lax.fori_loop(first, last, add, (jnp.zeros((6, TILE), F32),) * owned)
             for block in range(owned):
-                grad_ref[:, block * BLOCK + start : block * BLOCK + start + TILE] += sums[block]
+                columns = slice(block * BLOCK + start, block * BLOCK + start + TILE)
+                grad_ref[:, columns] = into(block, start, columns) + sums[block]
 
     all_first.wait_recv()
-    gather(0, groups)
+    gather(0, groups, lambda block, start, columns: local_ref[block, 0:6, start : start + TILE])
     all_along.wait_recv()
     total = lax.fori_loop(1, groups, lambda r, kept: kept + along_ref[r], along_ref[0])
     energy_ref[0, 0] = jnp.max(total)
     all_last.wait_recv()
-    gather(groups, 2 * groups)
+    gather(groups, 2 * groups, lambda block, start, columns: grad_ref[:, columns])
     for copies in (all_asks, all_near, all_far, all_twin, all_first, all_last, all_across, all_along):
         copies.wait_send()
 
@@ -440,7 +433,7 @@
             pltpu.VMEM((groups - near, 7, BLOCK), F32),
             pltpu.VMEM((groups, 7, BLOCK), F32),
             pltpu.VMEM((7, BLOCK), F32),
-            pltpu.VMEM((groups, 32, BLOCK), F32),
+            pltpu.VMEM((32, BLOCK), F32),
             pltpu.VMEM((groups + 1, 6, BLOCK), F32),
             pltpu.VMEM((slots, 6, BLOCK), F32),
             pltpu.VMEM((slots, 6, BLOCK), F32),
@@ -452,6 +445,7 @@
             pltpu.VMEM((DEPTH * TILE, TILE), BF16),
             pltpu.VMEM((64, TILE), BF16),
             pltpu.VMEM((32, BLOCK), F32),
+            pltpu.VMEM((owned, 8, BLOCK), F32),
             pltpu.SemaphoreType.DMA((8,)),
             pltpu.SemaphoreType.DMA((8,)),
             pltpu.SemaphoreType.DMA,

time: 122 us -> 122 us (level)
  no operation moved by 1% of the time
where the time goes in v5:
time: 122 us
  Pallas kernels  114 us (93%)
  local copies, waits for them, and re-layouts  3.69 us (3%)
  between operations  3.1 us (3%)
  other arithmetic  1.39 us (1%)
    pallas_call x1, Pallas kernels, shards(): pl.pallas_call(pair_kernel, out_shape=[jax.ShapeDtypeStruct((6, owned * B...  114 us
    unnamed x7, local copies, waits for them, and re-layouts  2.96 us

profile of v5, /device:TPU:1, one launch (start us, length us, event | category | flops | bytes accessed | tf_op | source)
XLA Modules:
  0.0 121.8 jit_solution(2310474378474136892)
XLA Ops:
  1.3 0.0 copy-start.1
  1.3 0.6 copy-done.1
  1.9 0.2 convert_reduce_fusion.1
  2.1 0.0 copy-start
  2.1 0.0 copy-start.2
  2.2 0.6 copy-done
  2.8 0.0 copy-done.2
  2.8 0.2 convert_reduce_fusion
  3.0 0.1 select_reduce_fusion.1
  3.1 0.1 select_reduce_fusion
  3.3 0.7 concatenate.3.plan_ref
  3.9 0.1 fusion.6
  4.0 0.7 broadcast_select_fusion.1.want_ref
  4.7 113.7 %shard_map.68 = (f32[6,8192]{1,0:T(8,128)}, f32[1,1]{1,0:T(1,128)}) custom-call(s32[224]{0:T(256)} %concatenate.3.plan_ref, s32[32,1,128]{2,1,0:T(1,128)} %broadcast_select_fusion.1.want_ref, f32[7,8192]{1,0:T(8,128)} %features_ref.1), custom_call_target="tpu_custom_call" | custom-call | tf_op jit(solution)/shard_map/pallas_call | solution.py:417
  118.4 1.7 %copy.10 = f32[6,8192]{1,0:T(8,128)} copy(f32[6,8192]{1,0:T(8,128)} %get-tuple-element.22) | data formatting | bytes 393216
  (5 shorter events, 0.0 us)
Async XLA Ops:
  1.3 0.7 copy-start.1
  2.1 0.7 copy-start
  2.1 0.7 copy-start.2

commit v6 on v5

--- a/solution.py
+++ b/solution.py
@@ -101,7 +101,7 @@
     grad_ref, energy_ref,
     block_ref, left_ref, moment_ref, ask_ref, asked_ref, out_ref,
     near_ref, far_ref, twin_ref, now_ref, mine_ref, result_ref, back_ref, home_ref,
-    share_ref, across_ref, along_ref, past_ref, high_ref, low_ref, column_ref, partial_ref, local_ref,
+    share_ref, across_ref, along_ref, past_ref, high_ref, low_ref, column_ref, partial_ref, local_ref, sums_ref,
     send_sem, recv_sem, local_sem,
 ):
     groups = want_ref.shape[0]
@@ -113,14 +113,23 @@
     my_row = lax.axis_index("gx")
 
     def offset(r):
-        half, odd = (r + 1) // 2, lax.rem(r, 2)
-        return odd * half + (1 - odd) * (groups - half)
+        if groups != 32:
+            half, odd = (r + 1) // 2, lax.rem(r, 2)
+            return odd * half + (1 - odd) * (groups - half)
+        core = lax.rem(r, 2)
+        ring = lax.rem(r // 2 + 4, 9)
+        close = 8 * (ring // 3) + 2 * lax.rem(ring, 3) - 10 + core
+        rest = jnp.maximum(r - 18, 0)
+        across_z = 14 + 2 * (rest // 2) + core
+        across_x = 8 * (jnp.maximum(rest - 8, 0) // 2) - 4 + core
+        beyond, last = r // 18, rest // 8
+        return 32 + (1 - beyond) * close + beyond * ((1 - last) * across_z + last * across_x)
 
     def ahead(r):
         return {"gy": lax.rem(me + offset(r), groups)}
 
     def behind(r):
-        return {"gy": lax.rem(me + 2 * groups - offset(r), groups)}
+        return {"gy": lax.rem(me + 3 * groups - offset(r), groups)}
 
     def remote(kind, source, target, device):
         return pltpu.make_async_remote_copy(
@@ -226,6 +235,7 @@
     all_near.wait_recv()
 
     tiles = BLOCK // TILE
+    width, piece = BLOCK - BLOCK // 4, BLOCK // 8
     chunks = tiles * tiles
 
     def cut(index):
@@ -247,11 +257,27 @@
         first = moment_ref[plan_ref[entry], :, rows]
         return last_column + second_terms(first, high, low)
 
+    def pack(entry, out):
+        result_ref[entry, 0:6] = out[0:6, :width]
+        for part in range(6):
+            top, start = 2 * (part % 3), width + (part // 3) * piece
+            result_ref[entry, 6:8, part * piece : (part + 1) * piece] = out[top : top + 2, start : start + piece]
+
+    def unpack(block):
+        start = block * BLOCK
+        local_ref[block, 0:6, :width] += sums_ref[block, 0:6]
+        for part in range(6):
+            top, place = 2 * (part % 3), width + (part // 3) * piece
+            local_ref[block, top : top + 2, place : place + piece] += sums_ref[
+                block, 6:8, part * piece : (part + 1) * piece
+            ]
+        grad_ref[:, start : start + BLOCK] = local_ref[block, 0:6]
+
     def conclude(entry, last_column):
         moments = jnp.concatenate([partial_ref[:, : BLOCK - TILE], last_column], axis=1)
         factor = plan_ref[6 * groups + entry].astype(F32)
         out, share = finish(read_rows(past_ref[...]), moments, factor)
-        result_ref[entry] = out[0:6]
+        pack(entry, out)
         block = plan_ref[entry]
         out, _ = finish(read_rows(block_ref[block]), mine_ref[...], factor)
         for own in range(owned):
@@ -338,11 +364,12 @@
     share_ref[0] = jnp.full(share_ref.shape[1:], jnp.sum(energy) * (1.0 / BLOCK), F32)
     each(1, rows_x, lambda r: share_across(r).start())
 
-    def send_last(r):
+    def send_last(turn):
+        r = 1 + lax.rem(12 * turn, groups - 1)
         back_ref[groups + r] = result_ref[plan_ref[3 * groups + r]]
         give_back(1, r).start()
 
-    each(1, groups // 2, send_last)
+    each(0, groups // 2, send_last)
     all_across.wait_recv()
     across_ref[my_row] = share_ref[0]
     total = across_ref[0]
@@ -351,33 +378,43 @@
     share_ref[1] = total
     each(1, groups, lambda r: share_along(r).start())
     along_ref[me] = total
-    each(groups // 2, groups, send_last)
+    each(groups // 2, groups - 1, send_last)
     back_ref[groups] = result_ref[plan_ref[3 * groups]]
     home_ref[0] = back_ref[0]
     home_ref[groups] = back_ref[groups]
 
-    def gather(first, last, into):
-        for start in range(0, BLOCK, TILE):
+    def gather(first, last):
+        for start in range(0, width, TILE):
 
             def add(slot, sums, start=start):
-                piece = home_ref[slot, :, start : start + TILE]
+                part = home_ref[slot, :, start : start + TILE]
                 wish = asked_ref[lax.rem(slot, groups), 0, slot // groups]
-                return tuple(kept + jnp.where(wish == block, piece, 0.0) for block, kept in enumerate(sums))
-
-            sums = lax.fori_loop(first, last, add, (jnp.zeros((6, TILE), F32),) * owned)
+                return tuple(kept + jnp.where(wish == block, part, 0.0) for block, kept in enumerate(sums))
+
+            sums = lax.fori_loop(first, last, add, (jnp.zeros((8, TILE), F32),) * owned)
             for block in range(owned):
-                columns = slice(block * BLOCK + start, block * BLOCK + start + TILE)
-                grad_ref[:, columns] = into(block, start, columns) + sums[block]
-
+                sums_ref[block, :, start : start + TILE] += sums[block]
+
+    sums_ref[...] = jnp.zeros_like(sums_ref)
     all_first.wait_recv()
-    gather(0, groups, lambda block, start, columns: local_ref[block, 0:6, start : start + TILE])
+    gather(0, groups)
     all_along.wait_recv()
     total = lax.fori_loop(1, groups, lambda r, kept: kept + along_ref[r], along_ref[0])
     energy_ref[0, 0] = jnp.max(total)
     all_last.wait_recv()
-    gather(groups, 2 * groups, lambda block, start, columns: grad_ref[:, columns])
+    gather(groups, 2 * groups)
+    for block in range(owned):
+        unpack(block)
     for copies in (all_asks, all_near, all_far, all_twin, all_first, all_last, all_across, all_along):
         copies.wait_send()
+
+
+def partner_order(groups):
+    if groups != 32:
+        return [(r + 1) // 2 if r % 2 else (groups - r // 2) % groups for r in range(groups)]
+    close = [8 * (m // 3 - 1) + 2 * (m % 3 - 1) for m in [4, 5, 6, 7, 8, 0, 1, 2, 3]]
+    wide = [16 + 2 * dx for dx in (-1, 0, 1, 2)] + [4 + 8 * dz for dz in (-1, 0, 1)]
+    return [(base + core) % groups for base in close + wide for core in (0, 1)]
 
 
 def shards(features, first_slot, second_owner, second_slot, pair_count):
@@ -395,7 +432,10 @@
     factors = jnp.where(live, factors, 0)
     rank = jnp.sum((owners[:, None] == owners[None, :]) & (order[None, :] < order[:, None]), axis=1)
     ahead = lax.rem(owners - me + groups, groups)
-    distance = jnp.where(ahead <= groups // 2, jnp.maximum(2 * ahead - 1, 0), 2 * (groups - ahead))
+    offsets = jnp.asarray(partner_order(groups), jnp.int32)
+    distance = jnp.sum(
+        jnp.where(ahead[:, None] == offsets[None, :], jnp.arange(groups, dtype=jnp.int32)[None, :], 0), axis=1
+    )
     key = rank.astype(jnp.int32) * groups + distance
     place = jnp.sum(key[None, :] < key[:, None], axis=1).astype(jnp.int32)
     at_step = place[None, :] == order[:, None]
@@ -434,9 +474,9 @@
             pltpu.VMEM((groups, 7, BLOCK), F32),
             pltpu.VMEM((7, BLOCK), F32),
             pltpu.VMEM((32, BLOCK), F32),
-            pltpu.VMEM((groups + 1, 6, BLOCK), F32),
-            pltpu.VMEM((slots, 6, BLOCK), F32),
-            pltpu.VMEM((slots, 6, BLOCK), F32),
+            pltpu.VMEM((groups + 1, 8, BLOCK - BLOCK // 4), F32),
+            pltpu.VMEM((slots, 8, BLOCK - BLOCK // 4), F32),
+            pltpu.VMEM((slots, 8, BLOCK - BLOCK // 4), F32),
             pltpu.VMEM((2, 8, 128), F32),
             pltpu.VMEM((lax.axis_size("gx"), 8, 128), F32),
             pltpu.VMEM((groups, 8, 128), F32),
@@ -446,6 +486,7 @@
             pltpu.VMEM((64, TILE), BF16),
             pltpu.VMEM((32, BLOCK), F32),
             pltpu.VMEM((owned, 8, BLOCK), F32),
+            pltpu.VMEM((owned, 8, BLOCK - BLOCK // 4), F32),
             pltpu.SemaphoreType.DMA((8,)),
             pltpu.SemaphoreType.DMA((8,)),
             pltpu.SemaphoreType.DMA,

time: 122 us -> 119 us (0.975)
  Pallas kernels: 114 us -> 110 us
    pallas_call x1, Pallas kernels: 114 us -> 110 us  [shards(): pl.pallas_call(pair_kernel, out_shape=[jax.ShapeDtypeStruct((6, owned * B...]
    unnamed x7 -> x9, local copies, waits for them, and re-layouts: 2.96 us -> 3.63 us
where the time goes in v6:
time: 119 us; the launch traced here: 118 us
  Pallas kernels  110 us (92%)
  local copies, waits for them, and re-layouts  4.36 us (4%)
  between operations  3.1 us (3%)
  other arithmetic  1.38 us (1%)
    pallas_call x1, Pallas kernels, shards(): pl.pallas_call(pair_kernel, out_shape=[jax.ShapeDtypeStruct((6, owned * B...  110 us
    unnamed x9, local copies, waits for them, and re-layouts  3.63 us

profile of v6, /device:TPU:1, one launch (start us, length us, event | category | flops | bytes accessed | tf_op | source)
XLA Modules:
  0.0 118.4 jit_solution(16540467364421537605)
XLA Ops:
  1.3 0.0 copy-start
  1.3 0.6 copy-done
  1.9 0.0 copy-start.1
  1.9 0.0 copy-start.2
  1.9 0.6 copy-done.1
  2.6 0.0 copy-done.2
  2.6 0.0 copy-start.3
  2.6 0.7 copy-done.3
  3.3 0.2 select_reduce_fusion.5
  3.5 0.2 convert_reduce_fusion
  3.7 0.1 select_reduce_fusion.1
  3.8 0.1 select_reduce_fusion
  3.9 0.7 concatenate.3.plan_ref
  4.6 0.1 fusion.3
  4.7 0.7 broadcast_select_fusion.1.want_ref
  5.4 109.6 %shard_map.77 = (f32[6,8192]{1,0:T(8,128)}, f32[1,1]{1,0:T(1,128)}) custom-call(s32[224]{0:T(256)} %concatenate.3.plan_ref, s32[32,1,128]{2,1,0:T(1,128)} %broadcast_select_fusion.1.want_ref, f32[7,8192]{1,0:T(8,128)} %features_ref.1), custom_call_target="tpu_custom_call" | custom-call | tf_op jit(solution)/shard_map/pallas_call | solution.py:457
  115.0 1.7 %copy.11 = f32[6,8192]{1,0:T(8,128)} copy(f32[6,8192]{1,0:T(8,128)} %get-tuple-element.21) | data formatting | bytes 393216
  (7 shorter events, 0.0 us)
Async XLA Ops:
  1.3 0.7 copy-start
  1.9 0.7 copy-start.1
  1.9 0.7 copy-start.2
  2.6 0.7 copy-start.3

commit v7 on v6

--- a/solution.py
+++ b/solution.py
@@ -97,9 +97,9 @@
 
 
 def pair_kernel(
-    plan_ref, want_ref, features_ref,
+    plan_ref, features_ref,
     grad_ref, energy_ref,
-    block_ref, left_ref, moment_ref, ask_ref, asked_ref, out_ref,
+    want_ref, block_ref, left_ref, moment_ref, ask_ref, asked_ref, out_ref,
     near_ref, far_ref, twin_ref, now_ref, mine_ref, result_ref, back_ref, home_ref,
     share_ref, across_ref, along_ref, past_ref, high_ref, low_ref, column_ref, partial_ref, local_ref, sums_ref,
     send_sem, recv_sem, local_sem,
@@ -192,6 +192,13 @@
 
     each(1, groups, greet)
     each(1, rows_x, greet_across)
+    lane = lax.broadcasted_iota(jnp.int32, (1, 128), 1)
+
+    def list_wants(r):
+        twin_want = jnp.where(lane == 1, plan_ref[5 * groups + r], 0)
+        want_ref[r] = jnp.where(lane == 0, plan_ref[4 * groups + r], twin_want)
+
+    each(0, groups, list_wants)
     for block in range(owned):
         block_ref[block] = features_ref[:, block * BLOCK : (block + 1) * BLOCK]
     pl.semaphore_wait(barrier, groups - 1 + rows_x - 1)
@@ -449,8 +456,6 @@
     plan = jnp.concatenate(
         [pick(at_step, first_slot), pick(at_step, key), serve, want, pick(at_step, factors)]
     ).astype(jnp.int32)
-    lane = jnp.arange(128, dtype=jnp.int32)[None, :]
-    asked = jnp.where(lane == 0, want[:groups, None], jnp.where(lane == 1, want[groups:, None], 0))
 
     smem = pl.BlockSpec(memory_space=pltpu.SMEM)
     vmem = pl.BlockSpec(memory_space=pltpu.VMEM)
@@ -460,9 +465,10 @@
             jax.ShapeDtypeStruct((6, owned * BLOCK), F32),
             jax.ShapeDtypeStruct((1, 1), F32),
         ],
-        in_specs=[smem, vmem, vmem],
+        in_specs=[smem, vmem],
         out_specs=[vmem, smem],
         scratch_shapes=[
+            pltpu.VMEM((groups, 1, 128), jnp.int32),
             pltpu.VMEM((owned, 7, BLOCK), F32),
             pltpu.VMEM((owned, BLOCK, 48), BF16),
             pltpu.VMEM((owned, 64, BLOCK), BF16),
@@ -494,7 +500,7 @@
         compiler_params=pltpu.CompilerParams(
             vmem_limit_bytes=56 * 2**20, collective_id=0, has_side_effects=True
         ),
-    )(plan, asked.reshape(groups, 1, 128), features)
+    )(plan, features)
     return (gradient, energy.reshape(()))
 
 

time: 119 us -> 118 us (level)
  no operation moved by 1% of the time
where the time goes in v7:
time: 118 us
  Pallas kernels  110 us (93%)
  local copies, waits for them, and re-layouts  4.28 us (4%)
  between operations  3.08 us (3%)
    pallas_call x1, Pallas kernels, shards(): pl.pallas_call(pair_kernel, out_shape=[jax.ShapeDtypeStruct((6, owned * B...  110 us
    unnamed x9, local copies, waits for them, and re-layouts  3.63 us

profile of v7, /device:TPU:1, one launch (start us, length us, event | category | flops | bytes accessed | tf_op | source)
XLA Modules:
  0.0 117.6 jit_solution(13656227762609759560)
XLA Ops:
  1.3 0.0 copy-start
  1.3 0.6 copy-done
  1.9 0.0 copy-start.1
  1.9 0.0 copy-start.2
  1.9 0.6 copy-done.1
  2.6 0.0 copy-done.2
  2.6 0.0 copy-start.3
  2.6 0.7 copy-done.3
  3.3 0.2 select_reduce_fusion.5
  3.5 0.2 convert_reduce_fusion
  3.7 0.1 select_reduce_fusion.1
  3.8 0.1 select_reduce_fusion
  3.9 0.6 concatenate.3.plan_ref
  4.6 109.6 %shard_map.77 = (f32[6,8192]{1,0:T(8,128)}, f32[1,1]{1,0:T(1,128)}) custom-call(s32[224]{0:T(256)} %concatenate.3.plan_ref, f32[7,8192]{1,0:T(8,128)} %features_ref.1), custom_call_target="tpu_custom_call" | custom-call | tf_op jit(solution)/shard_map/pallas_call | solution.py:462
  114.1 1.7 %copy.11 = f32[6,8192]{1,0:T(8,128)} copy(f32[6,8192]{1,0:T(8,128)} %get-tuple-element.17) | data formatting | bytes 393216
  (6 shorter events, 0.0 us)
Async XLA Ops:
  1.3 0.7 copy-start
  1.9 0.7 copy-start.1
  1.9 0.7 copy-start.2
  2.6 0.7 copy-start.3
